TPU v7x, 32 devices: a whole 2x2x4 slice. The times are simulated.
32 devices in a mesh: dp: 16 (over z, y, core), seq: 2 (over x).
Axes of the slice: x: 2, y: 2, z: 4, core: 2. Of those that a mesh axis runs over, the one named last changes fastest.
Arguments:
- tokens: bfloat16 [2, 16, 1408, 1280], P(None, 'dp', 'seq'), may hold values from -6 to 6
- cotangent: bfloat16 [2, 16, 1408, 1280], P(None, 'dp', 'seq'), may hold values from -6 to 6
- parents: int32 [2, 16, 44], P(None, 'dp'), may hold values from 0 to 43, as said below
- owners: int32 [122], replicated, may hold values from 0 to 15, as said below
- weight_store: float32 [256, 64, 1280], P('dp')
- gain_store: float32 [32, 1280], P('dp'), may hold values from 0.5 to 1.5
- weight_first: float32 [256, 64, 1280], P('dp')
- gain_first: float32 [32, 1280], P('dp'), may hold values from -1280 to 1280
- weight_second: float32 [256, 64, 1280], P('dp')
- gain_second: float32 [32, 1280], P('dp'), may hold values from 22528 to 360448
Outputs:
- mixed: bfloat16 [2, 16, 1408, 1280], P(None, 'dp', 'seq')
- token_grad: bfloat16 [2, 16, 1408, 1280], P(None, 'dp', 'seq')
- weight_new: float32 [256, 64, 1280], P('dp')
- gain_new: float32 [32, 1280], P('dp')
- weight_first_new: float32 [256, 64, 1280], P('dp')
- gain_first_new: float32 [32, 1280], P('dp')
- weight_second_new: float32 [256, 64, 1280], P('dp')
- gain_second_new: float32 [32, 1280], P('dp')
- weight_copies: bfloat16 [6, 1280, 1280], replicated
- gain_copies: bfloat16 [2, 1280], replicated
Inputs may be any that keep to these rules, and one draw needn't show every extreme that they name: `parents`: in every tree, segments 0 to 31 form the trunk: segment 0 is its own parent and each other trunk segment has the one before it as parent. The other 12 segments are 4 branches, each with a parent among trunk segments 32 // 2 to 31, and 8 leaves, two with each branch as parent. The last segment is always a branch; which of the others are branches and which are leaves is drawn from the seed. No index of dp owns more than 16 of the first 120 entries, and one owns exactly 16 in every draw; the last two entries are the owners of g1 and g2.
All inputs are finite; a program needn't handle non-finite values.
Results may differ from a plain program's by a relative error of at most 0.015.
Values may be sent and summed in bfloat16 or wider, within the bound.
A program may use at most 640 MiB of HBM per device.

v0:
```python
import functools

import jax
import jax.numpy as jnp
from jax import lax
from jax.experimental import pallas as pl
from jax.experimental.pallas import tpu as pltpu
from jax.sharding import Mesh
from jax.sharding import PartitionSpec as P

HEAD = 80
SEG = 32
TRUNK_SEGS = 32
ALWAYS_SEGS = TRUNK_SEGS // 2
STEP = 7
LANES = 128
WINDOW = 256
QUERY_BLOCK = 256

NORM_EPS = 1e-06
BETA_ONE = 0.5
BETA_TWO = 0.5
ADAM_EPS = 1e-08
MATRIX_DECAY = 0.1
RATE_QKV = 0.03
RATE_OUT = 0.4
RATE_GAIN = 0.4
MASKED = -1e30
SCALE = HEAD**-0.5
LOG2E = 1.4426950408889634
ALL = ("chip", "core", "seq")
NT = (((1,), (1,)), ((), ()))
TN = (((0,), (0,)), ((), ()))


def moved(value):
    chips = lax.axis_size("chip")
    pairs = [(k * 4 + c * 2 + 1 - c, k * 4 + 2 - 2 * c + c) for k in range(chips) for c in range(2)]
    return lax.ppermute(value, ALL, pairs)


def settled(value, arrived):
    return jnp.where(lax.axis_index("core") == lax.axis_index("seq"), value, arrived)


def transposed(value):
    return settled(value, moved(value))


def partner(value):
    return lax.ppermute(value, "core", [(0, 1), (1, 0)])


def owner_slots(owners, slot_dev):
    count = owners.shape[0] - 2
    piece_owner = owners[:count]
    labels = jnp.arange(count, dtype=jnp.int32)
    same = (piece_owner[:, None] == piece_owner[None, :]) & (labels[None, :] < labels[:, None])
    rank = jnp.sum(same.astype(jnp.int32), axis=1)
    return (piece_owner, rank)


def tail_limits(parents):
    up = parents[:, TRUNK_SEGS:]
    leaf = up >= TRUNK_SEGS
    above = jnp.where(leaf, up - TRUNK_SEGS, 0)
    labels = jnp.arange(up.shape[1], dtype=jnp.int32)
    hot = above[:, :, None] == labels[None, None, :]
    upper = jnp.sum(jnp.where(hot, up[:, None, :], 0), axis=2)
    attach = jnp.where(leaf, upper, up)
    limit = (attach + 1) * SEG
    branch = jnp.where(leaf, above, -1)
    return (jnp.repeat(limit, SEG, axis=1), jnp.repeat(branch, SEG, axis=1))


def query_blocks(length):
    trunk = TRUNK_SEGS * SEG
    blocks = []
    for first in range(0, trunk, QUERY_BLOCK):
        parts = [(0, first, "all")] if first else []
        blocks.append((first, QUERY_BLOCK, parts + [(first, QUERY_BLOCK, "causal")]))
    always = ALWAYS_SEGS * SEG
    tail = length - trunk
    blocks.append(
        (trunk, tail, [(0, always, "all"), (always, trunk - always, "trunk"), (trunk, tail, "tail")])
    )
    return blocks


def allowed_pairs(kind, key_first, key, query, limit, branch):
    if kind == "causal":
        return key <= query
    if kind == "trunk":
        return key + key_first < limit
    key_seg = key // SEG
    return ((key_seg == query // SEG) & (key <= query)) | (key_seg == branch)


def head_window(head, width):
    start = pl.multiple_of(
        jnp.minimum((head * HEAD) // LANES, width // LANES - WINDOW // LANES) * LANES, LANES
    )
    lane = lax.broadcasted_iota(jnp.int32, (1, WINDOW), 1) + start
    mine = (lane >= head * HEAD) & (lane < (head + 1) * HEAD)
    return (pl.ds(start, WINDOW), mine)


def scaled_query(rows, mine):
    return jnp.where(mine, rows.astype(jnp.float32) * (SCALE * LOG2E), 0.0).astype(jnp.bfloat16)


def attend_kernel(limit_ref, branch_ref, q_ref, k_ref, v_ref, out_ref, lse_ref):
    head = pl.program_id(1)
    window, mine = head_window(head, q_ref.shape[2])
    stat_lane = lax.broadcasted_iota(jnp.int32, (1, LANES), 1)
    values = jnp.where(mine, v_ref[0, :, window], 1)
    for first, count, parts in query_blocks(q_ref.shape[1]):
        rows = pl.ds(first, count)
        query = scaled_query(q_ref[0, rows, window], mine)
        scores = []
        for key_first, keys, kind in parts:
            raw = lax.dot_general(
                query, k_ref[0, pl.ds(key_first, keys), window], NT, preferred_element_type=jnp.float32
            )
            if kind != "all":
                ok = allowed_pairs(
                    kind,
                    key_first,
                    lax.broadcasted_iota(jnp.int32, (count, keys), 1),
                    lax.broadcasted_iota(jnp.int32, (count, keys), 0),
                    limit_ref[0],
                    branch_ref[0],
                )
                raw = jnp.where(ok, raw, MASKED)
            scores.append(raw)
        top = functools.reduce(jnp.maximum, [jnp.max(s, axis=1, keepdims=True) for s in scores])
        gained = 0.0
        for raw, (key_first, keys, kind) in zip(scores, parts):
            gained = gained + jnp.dot(
                jnp.exp2(raw - top).astype(jnp.bfloat16),
                values[key_first : key_first + keys],
                preferred_element_type=jnp.float32,
            )
        weight_sum = jnp.max(jnp.where(mine, 0.0, gained), axis=1, keepdims=True)
        gained = (gained * (1.0 / weight_sum)).astype(jnp.bfloat16)
        out_ref[0, rows, window] = jnp.where(mine, gained, out_ref[0, rows, window])
        lse_ref[0, rows, :] = jnp.where(
            stat_lane == head, top + jnp.log2(weight_sum), lse_ref[0, rows, :]
        )


def attend(qkv, limit, branch):
    micro, length, columns = qkv.shape
    width = columns // 3
    heads = width // HEAD
    tail = length - TRUNK_SEGS * SEG

    def part(index):
        return pl.BlockSpec((1, length, width), lambda m, h, index=index: (m, 0, index))

    column = pl.BlockSpec((1, tail, 1), lambda m, h: (m, 0, 0))
    return pl.pallas_call(
        attend_kernel,
        grid=(micro, heads),
        in_specs=[column, column, part(0), part(1), part(2)],
        out_specs=[
            pl.BlockSpec((1, length, width), lambda m, h: (m, 0, 0)),
            pl.BlockSpec((1, length, LANES), lambda m, h: (m, 0, 0)),
        ],
        out_shape=[
            jax.ShapeDtypeStruct((micro, length, width), jnp.bfloat16),
            jax.ShapeDtypeStruct((micro, length, LANES), jnp.float32),
        ],
        compiler_params=pltpu.CompilerParams(vmem_limit_bytes=48 << 20),
        cost_estimate=pl.CostEstimate(
            flops=micro * heads * length * length * WINDOW * 3,
            bytes_accessed=micro * length * width * 8,
            transcendentals=micro * heads * length * length // 2,
        ),
    )(limit[:, :, None], branch[:, :, None], qkv, qkv, qkv)


def attend_back_kernel(
    limit_ref, branch_ref, lse_ref, q_ref, k_ref, v_ref, g_ref, a_ref, out_ref, dk_sum, dv_sum
):
    head = pl.program_id(1)
    width = q_ref.shape[2]
    window, mine = head_window(head, width)

    @pl.when(head == 0)
    def clear():
        dk_sum[...] = jnp.zeros_like(dk_sum)
        dv_sum[...] = jnp.zeros_like(dv_sum)

    ones = jnp.ones((8, WINDOW), jnp.float32)
    for first, count, parts in query_blocks(q_ref.shape[1]):
        rows = pl.ds(first, count)
        query = jnp.where(mine, q_ref[0, rows, window], 0)
        scaled = scaled_query(q_ref[0, rows, window], mine)
        grad = jnp.where(mine, g_ref[0, rows, window], 0)
        lse = lse_ref[0, pl.ds(head, 1), rows]
        gains = grad.astype(jnp.float32) * a_ref[0, rows, window].astype(jnp.float32)
        row_total = lax.dot_general(
            ones, gains, NT, precision=lax.Precision.HIGHEST, preferred_element_type=jnp.float32
        )[0:1]
        grad_query = 0.0
        for key_first, keys, kind in parts:
            where = pl.ds(key_first, keys)
            raw = lax.dot_general(
                k_ref[0, where, window], scaled, NT, preferred_element_type=jnp.float32
            )
            prob = jnp.exp2(raw - lse)
            if kind != "all":
                ok = allowed_pairs(
                    kind,
                    key_first,
                    lax.broadcasted_iota(jnp.int32, (keys, count), 0),
                    lax.broadcasted_iota(jnp.int32, (keys, count), 1),
                    limit_ref[0],
                    branch_ref[0],
                )
                prob = jnp.where(ok, prob, 0.0)
            grad_prob = lax.dot_general(
                v_ref[0, where, window], grad, NT, preferred_element_type=jnp.float32
            )
            grad_raw = (prob * (grad_prob - row_total)).astype(jnp.bfloat16)
            dv_sum[where, window] += jnp.dot(
                prob.astype(jnp.bfloat16), grad, preferred_element_type=jnp.float32
            )
            dk_sum[where, window] += jnp.dot(grad_raw, query, preferred_element_type=jnp.float32)
            grad_query = grad_query + lax.dot_general(
                grad_raw, k_ref[0, where, window], TN, preferred_element_type=jnp.float32
            )
        out_ref[0, rows, window] = jnp.where(
            mine, (grad_query * SCALE).astype(jnp.bfloat16), out_ref[0, rows, window]
        )

    @pl.when(head == pl.num_programs(1) - 1)
    def write():
        out_ref[0, :, pl.ds(width, width)] = (dk_sum[...] * SCALE).astype(jnp.bfloat16)
        out_ref[0, :, pl.ds(2 * width, width)] = dv_sum[...].astype(jnp.bfloat16)


def attend_back(qkv, grad, attended, lse, limit, branch):
    micro, length, columns = qkv.shape
    width = columns // 3
    heads = width // HEAD
    tail = length - TRUNK_SEGS * SEG

    def part(index):
        return pl.BlockSpec((1, length, width), lambda m, h, index=index: (m, 0, index))

    row = pl.BlockSpec((1, 1, tail), lambda m, h: (m, 0, 0))
    return pl.pallas_call(
        attend_back_kernel,
        grid=(micro, heads),
        in_specs=[
            row,
            row,
            pl.BlockSpec((1, heads, length), lambda m, h: (m, 0, 0)),
            part(0),
            part(1),
            part(2),
            part(0),
            part(0),
        ],
        out_specs=pl.BlockSpec((1, length, columns), lambda m, h: (m, 0, 0)),
        out_shape=jax.ShapeDtypeStruct((micro, length, columns), jnp.bfloat16),
        scratch_shapes=[pltpu.VMEM((length, width), jnp.float32)] * 2,
        compiler_params=pltpu.CompilerParams(vmem_limit_bytes=56 << 20),
        cost_estimate=pl.CostEstimate(
            flops=micro * heads * length * length * WINDOW * 7,
            bytes_accessed=micro * length * width * 14,
            transcendentals=micro * heads * length * length // 2,
        ),
    )(limit[:, None, :], branch[:, None, :], lse, qkv, qkv, qkv, grad, attended)


def norm_back(grad_normed, normed_unit, scale_rows, gain_row):
    scaled_grad = grad_normed * gain_row
    return scale_rows * (
        scaled_grad - normed_unit * jnp.mean(scaled_grad * normed_unit, axis=-1, keepdims=True)
    )


def adam_update(master, first, second, grad, rate, decay):
    first_new = BETA_ONE * first + (1.0 - BETA_ONE) * grad
    second_new = BETA_TWO * second + (1.0 - BETA_TWO) * grad * grad
    fix_one = 1.0 - BETA_ONE**STEP
    fix_two = 1.0 - BETA_TWO**STEP
    step_size = first_new / fix_one / (jnp.sqrt(second_new / fix_two) + ADAM_EPS)
    return (master - rate * (step_size + decay * master), first_new, second_new)


def product(left, right, spec):
    return jnp.einsum(spec, left, right, preferred_element_type=jnp.float32)


Y_CHIPS = 2
CAPACITY = 8
SPARE = 8
GROUP = 16
CHUNK = 256
MESH_IDS = pl.DeviceIdType.MESH


def place():
    chip = lax.axis_index("chip")
    return (
        chip // Y_CHIPS,
        lax.rem(chip, Y_CHIPS),
        lax.axis_index("core"),
        lax.axis_index("seq"),
        lax.axis_size("chip") // Y_CHIPS,
    )


def at_z(z, y):
    return {"chip": z * Y_CHIPS + y}


def ahead(d):
    z, y, core, x, depth = place()
    return at_z(lax.rem(z + d, depth), y)


def across(axis):
    z, y, core, x, _ = place()
    return {"y": at_z(z, 1 - y), "x": {"seq": 1 - x}, "core": {"core": 1 - core}}[axis]


def greet():
    depth = place()[4]
    barrier = pltpu.get_barrier_semaphore()
    peers = [ahead(d) for d in range(1, depth)] + [across("y"), across("x"), across("core")]
    for peer in peers:
        pl.semaphore_signal(barrier, inc=1, device_id=peer, device_id_type=MESH_IDS)
    pl.semaphore_wait(barrier, len(peers))


def sem_pair(*shape):
    return [pltpu.SemaphoreType.DMA(shape), pltpu.SemaphoreType.DMA(shape)]


def remote(source, target, sems, index, device):
    return pltpu.make_async_remote_copy(
        src_ref=source,
        dst_ref=target,
        send_sem=sems[0].at[index],
        recv_sem=sems[1].at[index],
        device_id=device,
        device_id_type=MESH_IDS,
    )


def total(*parts):
    return functools.reduce(jnp.add, [p.astype(jnp.float32) for p in parts]).astype(jnp.bfloat16)


class Flow:
    def __init__(self):
        self.sent = []

    def push(self, source, target, sems, index, device):
        copy = remote(source, target, sems, index, device)
        copy.start()
        self.sent.append(copy)

    def arrive(self, here, sems, index):
        remote(here, here, sems, index, across("core")).wait_recv()

    def drain(self):
        for copy in self.sent:
            copy.wait_send()


class Total(Flow):
    def __init__(self, axes, sums, inbox, sems):
        super().__init__()
        self.axes, self.sums, self.inbox, self.sems = (axes, sums, inbox, sems)
        self.done = 0

    def begin(self, value):
        self.sums[0] = value
        self.push(self.sums.at[0], self.inbox.at[0], self.sems, (0,), across(self.axes[0]))

    def step(self):
        i = self.done
        self.done += 1
        self.arrive(self.inbox.at[i], self.sems, (i,))
        self.sums[i + 1] = self.sums[i] + self.inbox[i]
        here = self.sums.at[i + 1]
        if i + 1 < len(self.axes):
            self.push(here, self.inbox.at[i + 1], self.sems, (i + 1,), across(self.axes[i + 1]))
            return
        for d in range(1, place()[4]):
            self.push(here, self.inbox.at[i + d], self.sems, (i + d,), ahead(d))

    def result(self):
        last = len(self.axes)
        value = self.sums[last]
        for d in range(1, place()[4]):
            self.arrive(self.inbox.at[last - 1 + d], self.sems, (last - 1 + d,))
            value = value + self.inbox[last - 1 + d]
        self.drain()
        return value


def distances(depth):
    return sorted(range(1, depth), key=lambda d: min(d, depth - d))


def total_scratch(axes, depth, width):
    return [
        pltpu.VMEM((axes + 1, 8, width), jnp.float32),
        pltpu.VMEM((axes + depth - 1, 8, width), jnp.float32),
    ] + sem_pair(axes + depth - 1)


def spread_sems(depth):
    return sem_pair(depth) + sem_pair(depth) + sem_pair(depth, 2) + sem_pair(depth, 4)


class Spread(Flow):
    def __init__(self, window, second, sems):
        super().__init__()
        self.window = window
        self.second = second
        self.third = "x" if second == "y" else "y"
        self.sems = [(sems[2 * i], sems[2 * i + 1]) for i in range(4)]

    def where(self, d, second=False, third=False, other_core=False):
        z, y, core, x, depth = place()
        if second if self.second == "y" else third:
            y = 1 - y
        if third if self.second == "y" else second:
            x = 1 - x
        return self.window(lax.rem(z - d + depth, depth), y, 1 - core if other_core else core, x)

    def forward(self, stage, index, block, device):
        self.push(block, block, self.sems[stage], index, device)

    def begin(self):
        self.waiting = distances(place()[4])
        self.along_z()
        self.onward(0)

    def along_z(self):
        if self.waiting:
            d = self.waiting.pop(0)
            self.forward(0, (d,), self.where(0), ahead(d))

    def onward(self, d):
        block = self.where(d)
        self.forward(1, (d,), block, across(self.second))
        self.forward(2, (d, 0), block, across(self.third))
        self.forward(3, (d, 0), block, across("core"))

    def from_z(self, d):
        self.arrive(self.where(d), self.sems[0], (d,))
        self.along_z()
        self.onward(d)

    def from_second(self, d):
        block = self.where(d, True)
        self.arrive(block, self.sems[1], (d,))
        self.forward(2, (d, 1), block, across(self.third))
        self.forward(3, (d, 2), block, across("core"))

    def from_third(self, d):
        for second in range(2):
            block = self.where(d, bool(second), True)
            self.arrive(block, self.sems[2], (d, second))
            self.forward(3, (d, 2 * second + 1), block, across("core"))

    def finish(self):
        for d in range(place()[4]):
            for second in range(2):
                for third in range(2):
                    block = self.where(d, bool(second), bool(third), True)
                    self.arrive(block, self.sems[3], (d, 2 * second + third))
        self.drain()


def device_block(z, y, core, x):
    return ((z * Y_CHIPS + y) * 2 + core) * 2 + x


def chip_block(z, y, x):
    return (z * Y_CHIPS + y) * 2 + x


def gather_kernel(
    split,
    cut,
    block_ref,
    row_ref,
    spare_rank_ref,
    spare_mine_ref,
    low_ref,
    gain_ref,
    *refs,
):
    outs = refs[: 4 if split else 1]
    gain_out, whole, stage, stage_sem, spare, core_in, y_in, z_in, held = refs[len(outs) : len(outs) + 9]
    gain_sum, gain_in = refs[len(outs) + 9 : len(outs) + 11]
    sems = refs[len(outs) + 11 :]
    z, y, core, x, depth = place()
    piece, width = low_ref.shape[1:]
    half = CAPACITY // 2
    base = half * piece // GROUP
    me = device_block(z, y, core, x)
    per_piece = piece // GROUP
    for i in range(base):
        source = pl.ds(i % per_piece * GROUP, GROUP)
        whole[me, i] = low_ref[x * half + i // per_piece, source]
    greet()

    def window(first, count):
        return lambda *who: whole.at[device_block(*who), pl.ds(first, count)]

    flow_sems = 8
    early = Spread(window(0, cut), "y", sems[2 : 2 + flow_sems])
    late = Spread(window(cut, base - cut), "x", sems[10 : 10 + flow_sems])
    loose = Spread(window(base, 1), "x", sems[18 : 18 + flow_sems])
    gains = Total(["core", "y"], gain_sum, gain_in, sems[0:2])
    spare_sems = sems[26:32]
    spare_flow = Flow()
    early.begin()
    late.begin()
    gains.begin(gain_ref[...])
    count = SPARE // 2
    for i in range(count):
        found = low_ref[spare_rank_ref[x * count + i]]
        spare[pl.ds(i * piece, piece)] = jnp.where(spare_mine_ref[x * count + i] > 0, found, 0)
    rows = core_in.shape[0]

    def part(index, size):
        return pl.ds(pl.multiple_of(index * size, GROUP), size)

    spare_flow.push(spare.at[part(1 - core, rows)], core_in, spare_sems[0:2], (0,), across("core"))
    flows = [early, late]

    def from_z(d):
        for flow in flows:
            flow.from_z(d)

    def from_second(d):
        for flow in flows:
            flow.from_second(d)

    order = distances(depth)
    from_z(order[0])
    spare_flow.arrive(core_in, spare_sems[0:2], (0,))
    held[...] = total(spare[part(core, rows)], core_in[...])
    spare_flow.push(held.at[part(1 - y, rows // 2)], y_in, spare_sems[2:4], (0,), across("y"))
    gains.step()
    from_second(0)
    for i in range(1, depth - 1):
        from_z(order[i])
        if i == 1:
            spare_flow.arrive(y_in, spare_sems[2:4], (0,))
            y_in[...] = total(held[part(y, rows // 2)], y_in[...])
            for e in range(1, depth):
                to = part(lax.rem(z + e, depth), GROUP)
                spare_flow.push(y_in.at[to], z_in.at[e], spare_sems[4:6], (e,), ahead(e))
            gains.step()
        from_second(order[i - 1])
        for flow in flows:
            flow.from_third(([0] + order)[i - 1])
    for d in range(1, depth):
        spare_flow.arrive(z_in.at[d], spare_sems[4:6], (d,))
    whole[me, base] = total(y_in[part(z, GROUP)], *[z_in[d] for d in range(1, depth)])
    loose.begin()
    from_second(order[-1])
    gain_out[...] = gains.result()
    for d in order:
        loose.from_z(d)
    for flow in flows:
        flow.from_third(order[-2])
    for d in range(depth):
        loose.from_second(d)
    for flow in flows:
        flow.from_third(order[-1])
    for d in range(depth):
        loose.from_third(d)
    for flow in flows + [loose]:
        flow.finish()
    spare_flow.drain()

    buffers = stage.shape[0]
    per_chunk = CHUNK // GROUP
    narrow = width // 2
    copies = []
    for index in range(6 * width // CHUNK):
        matrix, first = divmod(index * CHUNK, width)
        slot = index % buffers
        if index >= buffers:
            copies[index - buffers].wait()
        thin = split and matrix < 3
        columns = pl.ds(pl.multiple_of(core * narrow, LANES), narrow) if thin else slice(None)
        count = narrow if thin else width

        def step(i, carry, index=index, slot=slot, columns=columns, count=count):
            for g in range(per_piece):
                at = index * per_chunk + i * per_piece + g
                target = pl.ds(pl.multiple_of(i * piece + g * GROUP, GROUP), GROUP)
                stage[slot, target, pl.ds(0, count)] = whole[block_ref[at], row_ref[at], :, columns]
            return carry

        lax.fori_loop(0, per_chunk // per_piece, step, 0)
        if thin:
            target = outs[0].at[pl.ds(first, CHUNK), pl.ds(matrix * narrow, narrow)]
        elif split:
            target = outs[matrix - 2].at[pl.ds(first, CHUNK)]
        else:
            target = outs[0].at[matrix, pl.ds(first, CHUNK)]
        copies.append(
            pltpu.make_async_copy(stage.at[slot, :, pl.ds(0, count)], target, stage_sem.at[slot])
        )
        copies[-1].start()
    for copy in copies[-buffers:]:
        copy.wait()


def gather_pieces(low, gains, plan, split):
    slots, piece, width = low.shape
    block, row, spare_rank, spare_mine, gain_mine = plan
    chips = lax.axis_size("chip")
    depth = chips // Y_CHIPS
    base = CAPACITY // 2 * piece // GROUP
    shapes = [(width, 3 * (width // 2))] + [(width, width)] * 3 if split else [(6, width, width)]
    lane = SPARE * piece // 4
    buffers = 4
    picked = jnp.where(gain_mine[:, None], gains[: gain_mine.shape[0]].astype(jnp.float32), 0.0)
    padded = jnp.concatenate([picked, jnp.zeros((6, width), jnp.float32)], axis=0)
    vmem = pl.BlockSpec(memory_space=pltpu.VMEM)
    smem = pl.BlockSpec(memory_space=pltpu.SMEM)
    outs = pl.pallas_call(
        functools.partial(gather_kernel, split, base // 4 if split else base // 2),
        in_specs=[smem] * 3 + [vmem] * 3,
        out_specs=[pl.BlockSpec(memory_space=pl.ANY)] * len(shapes) + [vmem],
        out_shape=[jax.ShapeDtypeStruct(s, jnp.bfloat16) for s in shapes]
        + [jax.ShapeDtypeStruct((8, width), jnp.float32)],
        scratch_shapes=[
            pltpu.VMEM((4 * chips, base + 1, GROUP, width), jnp.bfloat16),
            pltpu.VMEM((buffers, CHUNK, width), jnp.bfloat16),
            pltpu.SemaphoreType.DMA((buffers,)),
            pltpu.VMEM((2 * lane, width), jnp.bfloat16),
            pltpu.VMEM((lane, width), jnp.bfloat16),
            pltpu.VMEM((lane // 2, width), jnp.bfloat16),
            pltpu.VMEM((depth, GROUP, width), jnp.bfloat16),
            pltpu.VMEM((lane, width), jnp.bfloat16),
        ]
        + total_scratch(2, depth, width)
        + spread_sems(depth) * 3
        + sem_pair(1)
        + sem_pair(1)
        + sem_pair(depth),
        compiler_params=pltpu.CompilerParams(
            collective_id=0 if split else 1, has_side_effects=True, vmem_limit_bytes=48 << 20
        ),
        cost_estimate=pl.CostEstimate(
            flops=0, bytes_accessed=6 * width * width * 16, transcendentals=0
        ),
    )(
        block.reshape(-1),
        row.reshape(-1),
        spare_rank,
        jnp.broadcast_to(spare_mine[:, None, None], (SPARE, 1, width)),
        low,
        padded,
    )
    return (*outs[:-1], outs[-1][:2].astype(jnp.bfloat16))


def halves(matrices, split):
    if not split:
        return (matrices,)
    width = matrices.shape[1]
    narrow = width // 2
    thin = lax.dynamic_slice_in_dim(matrices[:3], lax.axis_index("core") * narrow, narrow, axis=2)
    side = jnp.concatenate([thin[0], thin[1], thin[2]], axis=1)
    return (side, matrices[3], matrices[4], matrices[5])


def gather_slots(low, gains, owners, split):
    slots, piece, width = low.shape
    piece_owner, rank = owner_slots(owners, slots)
    rows = slots * piece
    half = -(-(rows // 2 + 1) // GROUP) * GROUP
    filler = jnp.zeros((2 * half - rows - 2, width), jnp.bfloat16)
    packed = jnp.concatenate([low.reshape(rows, width), gains, filler], axis=0)
    share = lax.dynamic_slice_in_dim(packed, lax.axis_index("seq") * half, half, axis=0)
    groups = lax.all_gather(share, ALL, axis=0, tiled=True).reshape(-1, GROUP, width)
    per_owner = 2 * half // GROUP
    base = piece_owner * per_owner + rank * (piece // GROUP)
    index = base[:, None] + jnp.arange(piece // GROUP, dtype=jnp.int32)[None, :]
    matrices = groups[index.reshape(-1)].reshape(6, width, width)
    gain_rows = groups[owners[-2:] * per_owner + rows // GROUP][jnp.arange(2), jnp.arange(2)]
    return (*halves(matrices, split), gain_rows)


def kernels_fit(slots, piece, width):
    chips = lax.axis_size("chip")
    return slots == 2 * CAPACITY and piece == GROUP * (chips // Y_CHIPS) and width % CHUNK == 0


def spare_pieces(owners, slots):
    piece_owner, rank = owner_slots(owners, slots)
    spare = rank >= CAPACITY
    return (piece_owner, rank, spare, jnp.cumsum(spare.astype(jnp.int32)) - 1)


def gather_store(low, gains, owners, split, few):
    if not few:
        return gather_slots(low, gains, owners, split)
    slots, piece, width = low.shape
    dp_pos = lax.axis_index("chip") * 2 + lax.axis_index("core")
    piece_owner, rank, spare, order = spare_pieces(owners, slots)
    half = CAPACITY // 2
    groups = piece // GROUP
    group = jnp.arange(groups, dtype=jnp.int32)[None, :]
    block = jnp.where(
        spare[:, None],
        device_block(group, (order % 2)[:, None], ((order // 2) % 2)[:, None], (order // 4)[:, None]),
        (piece_owner * 2 + rank // half)[:, None],
    )
    row = jnp.where(spare[:, None], half * groups, (rank % half)[:, None] * groups + group)
    labels = jnp.arange(SPARE, dtype=jnp.int32)
    own = (spare & (piece_owner == dp_pos))[None, :] & (order[None, :] == labels[:, None])
    spare_rank = jnp.sum(jnp.where(own, rank[None, :], 0), axis=1)
    spare_mine = jnp.any(own, axis=1).astype(jnp.int32)
    plan = (block, row, spare_rank, spare_mine, owners[-2:] == dp_pos)
    return gather_pieces(low, gains, plan, split)


class Reduce(Flow):
    def __init__(self, first, shard, one, two, three, sems):
        super().__init__()
        self.first = first
        self.other = "y" if first == "x" else "x"
        self.shard = shard
        self.one, self.two, self.three = (one, two, three)
        self.sems = [sems[0:2], sems[2:4], sems[4:6]]

    def start(self, d, b):
        self.push(self.shard(d, b, 1), self.one.at[d, b], self.sems[0], (d, b), across(self.first))

    def from_first(self, d, b):
        here = self.one.at[d, b]
        self.arrive(here, self.sems[0], (d, b))
        here[...] = total(here[...], self.shard(d, b, 0)[...])
        if b:
            self.push(here, self.two.at[d], self.sems[1], (d,), across(self.other))

    def from_second(self, d):
        here = self.two.at[d]
        self.arrive(here, self.sems[1], (d,))
        here[...] = total(here[...], self.one[d, 0])
        if d:
            self.push(here, self.three.at[d], self.sems[2], (d,), ahead(d))

    def result(self):
        depth = place()[4]
        for d in range(1, depth):
            self.arrive(self.three.at[d], self.sems[2], (d,))
        value = total(self.two[0], *[self.three[d] for d in range(1, depth)])
        self.drain()
        return value


def reduce_kernel(
    source_ref,
    spare_ref,
    spare_mine_ref,
    early_ref,
    late_ref,
    gain_ref,
    slot_ref,
    gain_out,
    pieces,
    blocks,
    early_one,
    early_two,
    early_three,
    late_one,
    late_two,
    late_three,
    final,
    pair_in,
    full,
    full_in,
    spares,
    gain_sum,
    gain_in,
    load_sem,
    *sems,
):
    z, y, core, x, depth = place()
    narrow = pieces.shape[2]
    groups = late_ref.shape[1]
    per_block = blocks.shape[1]
    cut = early_one.shape[2]
    owned = CAPACITY // 2 * slot_ref.shape[1]
    order = distances(depth)[::-1] + [0]
    loads = []
    for matrix in range(3):
        columns = pl.ds(matrix * narrow, narrow)
        loads.append((early_ref.at[:, :, columns], matrix))
        loads.append((late_ref.at[matrix], matrix + 3))
    loads = [
        pltpu.make_async_copy(source, pieces.at[pl.ds(m * groups, groups)], load_sem.at[m])
        for source, m in loads
    ]
    for load in loads:
        load.start()
    pieces[6 * groups] = jnp.zeros((GROUP, narrow), jnp.bfloat16)
    greet()
    gains = Total(["core", "x", "y"], gain_sum, gain_in, sems[0:2])
    gains.begin(gain_ref[...])
    for load in loads:
        load.wait()

    def block_at(d, swap_y, swap_x):
        return chip_block(
            lax.rem(z + d, depth), 1 - y if swap_y else y, 1 - x if swap_x else x
        )

    early = Reduce(
        "x",
        lambda d, b, a: blocks.at[block_at(d, b, a), pl.ds(0, cut)],
        early_one,
        early_two,
        early_three,
        sems[2:8],
    )
    late = Reduce(
        "y",
        lambda d, b, a: blocks.at[block_at(d, a, b), pl.ds(cut, per_block - cut)],
        late_one,
        late_two,
        late_three,
        sems[8:14],
    )

    def fill(d, swap_y, swap_x):
        block = block_at(d, swap_y, swap_x)

        def step(i, carry):
            for g in range(2):
                blocks[block, 2 * i + g] = pieces[source_ref[block * per_block + 2 * i + g]]
            return carry

        lax.fori_loop(0, per_block // 2, step, 0)

    def start(d, b):
        for flow in (early, late):
            flow.start(d, b)

    fill(order[0], 1, 1)
    start(order[0], 1)
    fill(order[0], 0, 1)
    fill(order[0], 1, 0)
    start(order[0], 0)
    fill(order[0], 0, 0)
    for i, d in enumerate(order):
        later = order[i + 1] if i + 1 < len(order) else None
        if later is not None:
            fill(later, 1, 1)
        for flow in (early, late):
            flow.from_first(d, 1)
        if later is not None:
            start(later, 1)
            fill(later, 0, 1)
            fill(later, 1, 0)
        for flow in (early, late):
            flow.from_first(d, 0)
        if later is not None:
            start(later, 0)
            fill(later, 0, 0)
        if i:
            for flow in (early, late):
                flow.from_second(order[i - 1])
        if i < 3:
            gains.step()
    for flow in (early, late):
        flow.from_second(order[-1])
    final[pl.ds(0, cut)] = early.result()
    final[pl.ds(cut, per_block - cut)] = late.result()

    ends = Flow()
    own_spare = spares.at[z, y, x, core]
    ends.push(final.at[pl.ds((1 - core) * owned, owned)], pair_in, sems[14:16], (0,), across("core"))
    spares[z, y, x, core] = final[pl.ds(2 * owned, 2)]
    for d in range(1, depth):
        ends.push(own_spare, own_spare, sems[16:18], (d,), ahead(d))
    gain_out[...] = gains.result()
    ends.arrive(pair_in, sems[14:16], (0,))
    for g in range(owned):
        mine = final[core * owned + g]
        theirs = pair_in[g]
        first = core == 0
        full[g, :, pl.ds(pl.multiple_of(core * narrow, LANES), narrow)] = mine
        full[g, :, pl.ds(pl.multiple_of((1 - core) * narrow, LANES), narrow)] = theirs
    ends.push(full, full_in, sems[14:16], (1,), across("x"))
    for d in range(1, depth):
        from_z = spares.at[lax.rem(z - d + depth, depth), y, x, core]
        ends.arrive(from_z, sems[16:18], (d,))
    here = spares.at[:, y, x, core]
    ends.push(here, here, sems[14:16], (2,), across("y"))
    ends.arrive(spares.at[:, 1 - y, x, core], sems[14:16], (2,))
    here = spares.at[:, :, x, core]
    ends.push(here, here, sems[14:16], (3,), across("x"))
    ends.arrive(spares.at[:, :, 1 - x, core], sems[14:16], (3,))
    here = spares.at[:, :, :, core]
    ends.push(here, here, sems[14:16], (4,), across("core"))
    ends.arrive(spares.at[:, :, :, 1 - core], sems[14:16], (4,))
    ends.arrive(full_in, sems[14:16], (1,))
    per_piece = slot_ref.shape[1]
    half = CAPACITY // 2
    for i in range(half):
        for g in range(per_piece):
            slot_ref[x * half + i, g] = full[i * per_piece + g]
            slot_ref[(1 - x) * half + i, g] = full_in[i * per_piece + g]

    def pick(slot, carry):
        for g in range(per_piece):
            at = spare_ref[slot] * per_piece + g
            sub = spares.shape[4]
            chip = lax.div(at, 2 * sub)
            where = (lax.div(chip, Y_CHIPS), lax.rem(chip, Y_CHIPS), lax.rem(lax.div(at, sub), 2))
            for side in range(2):
                found = spares[(*where, side, lax.rem(at, sub))]
                slot_ref[CAPACITY + slot, g, :, pl.ds(side * narrow, narrow)] = jnp.where(
                    spare_mine_ref[slot] > 0, found, 0
                )
        return carry

    lax.fori_loop(0, slot_ref.shape[0] - CAPACITY, pick, 0)
    ends.drain()


def reduce_slots(early, late, gains, owners, slots, piece):
    width = late.shape[1]
    narrow = width // 2
    chips = lax.axis_size("chip")
    depth = chips // Y_CHIPS
    groups = width // GROUP
    per_piece = piece // GROUP
    dp_pos = lax.axis_index("chip") * 2 + lax.axis_index("core")
    piece_owner, rank, spare, order = spare_pieces(owners, slots)
    half = CAPACITY // 2
    labels = jnp.arange(piece_owner.shape[0], dtype=jnp.int32)
    empty = 6 * groups

    def groups_of(match):
        first = jnp.sum(jnp.where(match, labels, 0), axis=-1)[..., None] * per_piece
        groups_at = first + jnp.arange(per_piece, dtype=jnp.int32)
        return jnp.where(jnp.any(match, axis=-1)[..., None], groups_at, empty)

    block = jnp.arange(2 * chips, dtype=jnp.int32)[:, None]
    entry = jnp.arange(CAPACITY, dtype=jnp.int32)[None, :]
    owner_at = block // 2 * 2 + entry // half
    rank_at = block % 2 * half + entry % half
    base_groups = groups_of(
        (piece_owner == owner_at[..., None]) & (rank == rank_at[..., None])
    ).reshape(2 * chips, -1)
    spare_hot = spare & (order == jnp.arange(SPARE, dtype=jnp.int32)[:, None])
    spare_groups = groups_of(spare_hot).reshape(2 * chips, -1)
    source = jnp.concatenate([base_groups, spare_groups], axis=1)
    per_block = source.shape[1]
    mine = (piece_owner == dp_pos) & spare & (order < SPARE)
    slot_hot = mine & (rank == CAPACITY + jnp.arange(slots - CAPACITY, dtype=jnp.int32)[:, None])
    spare_at = jnp.sum(jnp.where(slot_hot, order, 0), axis=1)
    subs = SPARE * per_piece // (2 * chips)

    vmem = pl.BlockSpec(memory_space=pltpu.VMEM)
    smem = pl.BlockSpec(memory_space=pltpu.SMEM)
    hbm = pl.BlockSpec(memory_space=pl.ANY)
    cut = per_block // 4 + 1
    owned = half * per_piece
    padded = jnp.concatenate([gains, jnp.zeros((8 - gains.shape[0], width), jnp.float32)], axis=0)

    def group_block(*shape):
        return pltpu.VMEM(shape + (GROUP, narrow), jnp.bfloat16)

    def flow_blocks(count):
        return [group_block(depth, 2, count), group_block(depth, count), group_block(depth, count)]

    flow_sems = sem_pair(depth, 2) + sem_pair(depth) + sem_pair(depth)
    slot_grad, gain_sum = pl.pallas_call(
        reduce_kernel,
        in_specs=[smem] * 2 + [vmem, hbm, hbm, vmem],
        out_specs=[vmem, vmem],
        out_shape=[
            jax.ShapeDtypeStruct((slots, per_piece, GROUP, width), jnp.bfloat16),
            jax.ShapeDtypeStruct((8, width), jnp.float32),
        ],
        scratch_shapes=[group_block(6 * groups + 1), group_block(2 * chips, per_block)]
        + flow_blocks(cut)
        + flow_blocks(per_block - cut)
        + [
            group_block(per_block),
            group_block(owned),
            pltpu.VMEM((owned, GROUP, width), jnp.bfloat16),
            pltpu.VMEM((owned, GROUP, width), jnp.bfloat16),
            group_block(depth, Y_CHIPS, 2, 2, subs),
        ]
        + total_scratch(3, depth, width)[:2]
        + [pltpu.SemaphoreType.DMA((6,))]
        + total_scratch(3, depth, width)[2:]
        + flow_sems
        + flow_sems
        + sem_pair(5)
        + sem_pair(depth),
        compiler_params=pltpu.CompilerParams(
            collective_id=2, has_side_effects=True, vmem_limit_bytes=56 << 20
        ),
        cost_estimate=pl.CostEstimate(
            flops=0, bytes_accessed=6 * width * width * 8, transcendentals=0
        ),
    )(
        source.reshape(-1),
        spare_at,
        jnp.broadcast_to(jnp.any(slot_hot, axis=1).astype(jnp.int32)[:, None, None], (slots - CAPACITY, 1, narrow)),
        early.reshape(groups, GROUP, 3 * narrow),
        late.reshape(3, groups, GROUP, narrow),
        padded,
    )
    return (slot_grad.reshape(slots, piece, width), gain_sum[:2])


def reduce_all(early, late, gains, owners, slots, piece, few):
    if few:
        return reduce_slots(early, late, gains, owners, slots, piece)
    width = late.shape[1]
    narrow = width // 2
    dp_pos = lax.axis_index("chip") * 2 + lax.axis_index("core")
    pieces = owners.shape[0] - 2
    chips = lax.axis_size("chip")
    local = jnp.concatenate([jnp.transpose(early.reshape(width, 3, narrow), (1, 0, 2)), late], axis=0)
    share = lax.psum_scatter(
        local.reshape(6 * width, narrow), ("chip", "seq"), scatter_dimension=0, tiled=True
    )
    sums = lax.all_gather(share, ALL, axis=0, tiled=False).reshape(chips, 2, 2, -1, narrow)
    sums = jnp.transpose(sums, (0, 2, 3, 1, 4)).reshape(pieces, piece, width)
    piece_owner, rank = owner_slots(owners, slots)
    labels = jnp.arange(slots, dtype=jnp.int32)
    match = (piece_owner == dp_pos) & (rank == labels[:, None])
    slot_grad = jnp.where(jnp.any(match, axis=1)[:, None, None], sums[jnp.argmax(match, axis=1)], 0)
    return (slot_grad, lax.psum(gains, ALL))


def adam_kernel(rate_ref, master_ref, first_ref, second_ref, grad_ref, *outs):
    count = master_ref.shape[0]
    for i in range(count):
        new, first_new, second_new = adam_update(
            master_ref[i],
            first_ref[i],
            second_ref[i],
            grad_ref[i].astype(jnp.float32),
            rate_ref[pl.program_id(0) * count + i],
            MATRIX_DECAY,
        )
        outs[0][i] = new
        outs[1][i] = first_new
        outs[2][i] = second_new
        outs[3][i] = new.astype(jnp.bfloat16)


def adam_slots(master, first, second, grad, rate):
    slots, piece, width = master.shape
    count = min(slots, 2)
    block = pl.BlockSpec((count, piece, width), lambda i: (i, 0, 0))
    shape = jax.ShapeDtypeStruct(master.shape, jnp.float32)
    return pl.pallas_call(
        adam_kernel,
        grid=(slots // count,),
        in_specs=[pl.BlockSpec(memory_space=pltpu.SMEM)] + [block] * 4,
        out_specs=[block] * 4,
        out_shape=[shape] * 3 + [jax.ShapeDtypeStruct(master.shape, jnp.bfloat16)],
        compiler_params=pltpu.CompilerParams(vmem_limit_bytes=60 << 20),
        cost_estimate=pl.CostEstimate(
            flops=20 * slots * piece * width,
            bytes_accessed=28 * slots * piece * width,
            transcendentals=slots * piece * width,
        ),
    )(rate, master, first, second, grad)


def local(*arrays):
    owners, weight_store = arrays[3:5]
    if not kernels_fit(*weight_store.shape):
        return step(False, *arrays)
    order = spare_pieces(owners, weight_store.shape[0])[3]
    few = order[-1] < SPARE
    return lax.cond(few, functools.partial(step, True), functools.partial(step, False), *arrays)


def step(
    few,
    tokens,
    cotangent,
    parents,
    owners,
    weight_store,
    gain_store,
    weight_first,
    gain_first,
    weight_second,
    gain_second,
):
    core = lax.axis_index("core")
    dp_pos = lax.axis_index("chip") * 2 + core
    slot_dev, piece, width = weight_store.shape
    pieces = owners.shape[0] - 2
    piece_owner, rank = owner_slots(owners, slot_dev)
    gain_owner = owners[pieces:]
    micro, _, rows, _ = tokens.shape
    half = width // 2
    own_rows = core * rows
    own_columns = core * half

    def mine(value, axis, size, index):
        return lax.dynamic_slice_in_dim(value, index * size, size, axis=axis)

    limit, branch = tail_limits(transposed(parents[:, 0]))
    arrived = moved(tokens[:, 0])
    qkv_weight, out_weight, up_weight, down_weight, gain_low = gather_store(
        weight_store.astype(jnp.bfloat16), gain_store.astype(jnp.bfloat16), owners, True, few
    )
    gain_low, arrived, cot = lax.optimization_barrier((gain_low, arrived, cotangent[:, 0]))
    own_tokens = settled(tokens[:, 0], arrived)
    own_cot = transposed(cot)
    other_tokens = partner(own_tokens)

    def by_core(own, other, axis):
        return jnp.where(
            core == 0,
            jnp.concatenate([own, other], axis=axis),
            jnp.concatenate([other, own], axis=axis),
        )

    all_tokens = by_core(own_tokens, other_tokens, 1)
    gain_one = gain_low[0].astype(jnp.float32)
    gain_two = gain_low[1].astype(jnp.float32)

    def unit(values):
        scale = lax.rsqrt(jnp.mean(values * values, axis=-1, keepdims=True) + NORM_EPS)
        return (values * scale, scale)

    normed_one = (unit(all_tokens.astype(jnp.float32))[0] * gain_one).astype(jnp.bfloat16)
    normed_one = lax.optimization_barrier(normed_one)
    qkv = product(normed_one, qkv_weight, "mtd,de->mte").astype(jnp.bfloat16)
    attended_half, lse = attend(qkv, limit, branch)
    lse_rows = jnp.transpose(lse[:, :, : half // HEAD], (0, 2, 1))
    attended = by_core(
        mine(attended_half, 1, rows, core), partner(mine(attended_half, 1, rows, 1 - core)), 2
    )
    residual = own_tokens.astype(jnp.float32)
    hidden_one = residual + product(attended, out_weight, "mti,io->mto")
    unit_two, scale_two = unit(hidden_one)
    normed_two = (unit_two * gain_two).astype(jnp.bfloat16)
    up_rows = product(normed_two, up_weight, "mti,io->mto")
    sigmoid_up = jax.nn.sigmoid(up_rows)
    activated = (up_rows * sigmoid_up).astype(jnp.bfloat16)
    mixed_rows = (hidden_one + product(activated, down_weight, "mti,io->mto")).astype(jnp.bfloat16)
    mixed = transposed(mixed_rows)

    grad_down = product(activated, own_cot, "mti,mto->io")
    grad_hidden = product(own_cot, down_weight, "mto,io->mti")
    grad_up_rows = (grad_hidden * (sigmoid_up * (1.0 + up_rows * (1.0 - sigmoid_up)))).astype(
        jnp.bfloat16
    )
    grad_up = product(normed_two, grad_up_rows, "mti,mto->io")
    grad_normed_two = product(grad_up_rows, up_weight, "mto,io->mti")
    gain_two_grad = jnp.sum(grad_normed_two * unit_two, axis=(0, 1))
    grad_hidden_one = own_cot.astype(jnp.float32) + norm_back(
        grad_normed_two, unit_two, scale_two, gain_two
    )
    branch_grad = grad_hidden_one.astype(jnp.bfloat16)
    grad_out = product(attended, branch_grad, "mti,mto->io")
    late = jnp.stack([grad_out, grad_up, grad_down]).astype(jnp.bfloat16)
    late_back = partner(mine(late, 2, half, 1 - core))

    branch_grad, late = lax.optimization_barrier((branch_grad, late))
    grad_attended = product(branch_grad, out_weight, "mto,io->mti").astype(jnp.bfloat16)
    grad_half = by_core(
        mine(grad_attended, 2, half, core), partner(mine(grad_attended, 2, half, 1 - core)), 1
    )
    grad_qkv_rows = attend_back(qkv, grad_half, attended_half, lse_rows, limit, branch)
    grad_qkv = product(normed_one, grad_qkv_rows, "mti,mto->io")
    early = grad_qkv.astype(jnp.bfloat16)

    grad_normed_part = product(grad_qkv_rows, qkv_weight, "mte,de->mtd")
    grad_normed_one = mine(grad_normed_part, 1, rows, core) + partner(
        mine(grad_normed_part, 1, rows, 1 - core).astype(jnp.bfloat16)
    ).astype(jnp.float32)
    unit_one, scale_one = unit(residual)
    gain_one_grad = jnp.sum(grad_normed_one * unit_one, axis=(0, 1))
    token_rows = (
        grad_hidden_one + norm_back(grad_normed_one, unit_one, scale_one, gain_one)
    ).astype(jnp.bfloat16)
    token_grad = transposed(token_rows)
    gain_grads = jnp.stack([gain_one_grad, gain_two_grad])
    late = (mine(late, 2, half, core).astype(jnp.float32) + late_back.astype(jnp.float32)).astype(
        jnp.bfloat16
    )

    labels = jnp.arange(slot_dev, dtype=jnp.int32)
    match = (piece_owner[None, :] == dp_pos) & (rank[None, :] == labels[:, None])
    held = jnp.any(match, axis=1)
    piece_of = jnp.sum(jnp.where(match, jnp.arange(pieces, dtype=jnp.int32)[None, :], 0), axis=1)
    slot_grad, gain_sum = reduce_all(early, late, gain_grads, owners, slot_dev, piece, few)
    is_out = held & (piece_of // (width // piece) == 3)
    slot_rate = jnp.where(is_out, RATE_OUT, RATE_QKV).astype(jnp.float32)
    weight_new, weight_first_new, weight_second_new, weight_low = adam_slots(
        weight_store, weight_first, weight_second, slot_grad, slot_rate
    )
    gain_slot_grad = jnp.where((gain_owner == dp_pos)[:, None], gain_sum, 0.0)
    gain_new, gain_first_new, gain_second_new = adam_update(
        gain_store, gain_first, gain_second, gain_slot_grad, RATE_GAIN, 0.0
    )
    weight_copies, gain_copies = gather_store(
        weight_low, gain_new.astype(jnp.bfloat16), owners, False, few
    )
    return (
        mixed[:, None],
        token_grad[:, None],
        weight_new,
        gain_new,
        weight_first_new,
        gain_first_new,
        weight_second_new,
        gain_second_new,
        weight_copies,
        gain_copies,
    )


def solution(mesh):
    dp_count, seq_count = mesh.devices.shape
    fine = Mesh(mesh.devices.reshape(dp_count // 2, 2, seq_count), ALL)
    dp = ("chip", "core")
    rows = P(None, dp, "seq", None)
    store = P(dp, None, None)
    gains = P(dp, None)
    in_specs = (rows, rows, P(None, dp, None), P(), store, gains, store, gains, store, gains)
    out_specs = (rows, rows, store, gains, store, gains, store, gains, P(), P())
    return jax.shard_map(local, mesh=fine, in_specs=in_specs, out_specs=out_specs, check_vma=False)
```

profile of v0, /device:TPU:0, one launch (start us, length us, event | category | flops | bytes accessed | tf_op | source)
XLA Modules:
  0.0 868.7 jit_solution(17619900810390840342)
XLA Ops:
  9.4 835.8 %conditional.1 = (f32[16,64,1280]{2,1,0:T(8,128)}, f32[16,64,1280]{2,1,0:T(8,128)}, f32[16,64,1280]{2,1,0:T(8,128)}, bf16[2,1,704,1280]{3,2,0,1:T(8,128)(2,1)}, ...) conditional(s32[]{:T(128)} %bitcast.67, ...), branch_computations={%region_2.17_spmd, %region_17.38_spmd} | conditional | flops 164625940480 | bytes 1677977088 | solution.py:1098
  25.1 128.9 %branch_1_fun.6 = (bf16[1280,1920]{1,0:T(8,128)(2,1)}, bf16[1280,1280]{1,0:T(8,128)(2,1)S(1)}, bf16[1280,1280]{1,0:T(8,128)(2,1)}, bf16[1280,1280]{1,0:T(8,128)(2,1)}, f32[8,1280]{1,0:T(8,128)S(1)}) custom-call(s32[480]{0:T(512)S(1)} %reshape.615.block_ref, s32[480]{0:T(512)S(1)} %reshape.617.row_ref, s32[8]{0:T(128)S(1)} %get-tuple-element.295.spare_rank_ref, ...), custom_call_target="tpu_custom_call" | custom-call | bytes 157286400 | tf_op jit(solution)/shard_map/cond/branch_1_fun/pallas_call | solution.py:639
  167.7 7.0 fusion
  174.7 6.9 fusion.2
  184.7 17.1 %convolution_convert_fusion.q_ref.k_ref.v_ref = bf16[2,1408,1920]{2,1,0:T(8,128)(2,1)} fusion(bf16[2,1408,1280]{2,1,0:T(8,128)(2,1)S(1)} %fusion.2, bf16[1280,1920]{1,0:T(8,128)(2,1)S(1)} %bitcast.229), kind=kOutput, calls=%fused_computation.15 | convolution fusion | flops 13846609920 | bytes 22937600 | tf_op jit(solution)/shard_map/cond/branch_1_fun/mtd,de->mte/dot_general | solution.py:296
  201.7 52.2 %branch_1_fun.7 = (bf16[2,1408,640]{2,1,0:T(8,128)(2,1)S(1)}, f32[2,1408,128]{2,1,0:T(8,128)S(1)}) custom-call(s32[2,384,1]{2,1,0:T(8,128)S(1)} %reshape.697.limit_ref, s32[2,384,1]{2,1,0:T(8,128)S(1)} %reshape.698.branch_ref, bf16[2,1408,1920]{2,1,0:T(8,128)(2,1)} %convolution_convert_fusion.q_ref.k_ref.v_ref, ...), custom_call_target="tpu_custom_call" | custom-call | flops 24360517632 | bytes 14417920 | tf_op jit(solution)/shard_map/cond/branch_1_fun/pallas_call | solution.py:162
  264.0 8.7 %multiply_reduce_fusion.2 = (f32[2,704]{1,0:T(2,128)S(1)}, f32[2,704,1280]{2,1,0:T(8,128)S(1)}) fusion(bf16[1280,1280]{1,0:T(8,128)(2,1)S(1)} %copy-done.12, bf16[2,704,640]{2,1,0:T(8,128)(2,1)} %collective-permute-done.13, bf16[2,704,640]{2,1,0:T(8,128)(2,1)S(1)} %get-tuple-element.327, pred[]{:T(512)S(6)} %eq.149, ...), kind=kOutput, calls=%fused_computation.46 | convolution fusion | flops 4637161984 | bytes 17700352 | tf_op jit(solution)/shard_map/cond/branch_1_fun/mti,io->mto/dot_general | solution.py:296
  272.8 7.2 fusion.24
  280.0 9.6 %fusion.16 = bf16[1,1280,1280]{2,1,0:T(8,128)(2,1)} fusion(bf16[2,704,1280]{2,1,0:T(8,128)(2,1)S(1)} %broadcast_select_fusion, f32[2,704,1280]{2,1,0:T(8,128)} %fusion.24), kind=kOutput, calls=%fused_computation.47 | convolution fusion | flops 4624384000 | bytes 14090240 | tf_op jit(solution)/shard_map/cond/branch_1_fun/mti,mto->io/dot_general | solution.py:296
  289.6 9.3 %multiply_convert_fusion = bf16[2,704,1280]{2,1,0:T(8,128)(2,1)} fusion(f32[2,704,1280]{2,1,0:T(8,128)} %fusion.24, bf16[2,704,1280]{2,1,0:T(8,128)(2,1)S(1)} %broadcast_select_fusion, bf16[1280,1280]{1,0:T(8,128)(2,1)S(1)} %copy-done.93), kind=kOutput, calls=%fused_computation.41 | convolution fusion | flops 4629954560 | bytes 17694720 | tf_op jit(solution)/shard_map/cond/branch_1_fun/mto,io->mti/dot_general | solution.py:296
  298.9 9.4 %fusion.17 = bf16[1,1280,1280]{2,1,0:T(8,128)(2,1)} fusion(bf16[2,704,1280]{2,1,0:T(8,128)(2,1)} %multiply_convert_fusion, f32[2,704,1280]{2,1,0:T(8,128)S(1)} %get-tuple-element.338, f32[1280]{0:T(1024)S(1)} %get-tuple-element.293, f32[2,704]{1,0:T(2,128)S(1)} %add_rsqrt_fusion.2), kind=kOutput, calls=%fused_computation.48 | convolution fusion | flops 4620779520 | bytes 14100992 | tf_op jit(solution)/shard_map/cond/branch_1_fun/mti,mto->io/dot_general | solution.py:296
  308.3 10.7 %multiply_reduce_fusion = (f32[1280]{0:T(1024)S(1)}, f32[2,704]{1,0:T(2,128)S(1)}, f32[2,704,1280]{2,1,0:T(8,128)}) fusion(f32[2,704,1280]{2,1,0:T(8,128)S(1)} %get-tuple-element.338, f32[2,704]{1,0:T(2,128)S(1)} %add_rsqrt_fusion.2, f32[1280]{0:T(1024)S(1)} %get-tuple-element.293, bf16[2,704,1280]{2,1,0:T(8,128)(2,1)} %multiply_convert_fusion, ...), kind=kOutput, calls=%fused_computation.36 | convolution fusion | flops 4624545280 | bytes 21320704 | tf_op jit(solution)/shard_map/cond/branch_1_fun/mto,io->mti/dot_general | solution.py:296
  323.3 7.6 fusion.18
  352.8 101.7 %branch_1_fun.8 = bf16[2,1408,1920]{2,1,0:T(8,128)(2,1)} custom-call(s32[2,1,384]{2,1,0:T(1,128)} %reshape.695.limit_ref, s32[2,1,384]{2,1,0:T(1,128)} %reshape.696.branch_ref, f32[2,8,1408]{2,1,0:T(8,128)} %slice_bitcast_fusion.lse_ref, bf16[2,1408,1920]{2,1,0:T(8,128)(2,1)} %convolution_convert_fusion.q_ref.k_ref.v_ref, ...), custom_call_target="tpu_custom_call" | custom-call | flops 56841207808 | bytes 25231360 | tf_op jit(solution)/shard_map/cond/branch_1_fun/pallas_call | solution.py:254
  454.5 18.1 %fusion.19 = f32[2,1408,1280]{2,1,0:T(8,128)S(1)} fusion(bf16[2,1408,1920]{2,1,0:T(8,128)(2,1)} %branch_1_fun.8, bf16[1280,1920]{1,0:T(8,128)(2,1)S(1)} %bitcast.231), kind=kOutput, calls=%fused_computation.50 | convolution fusion | flops 13841203200 | bytes 30146560 | tf_op jit(solution)/shard_map/cond/branch_1_fun/mte,de->mtd/dot_general | solution.py:296
  482.8 13.8 %add_convert_fusion.1 = bf16[2,704,1280]{2,1,0:T(8,128)(2,1)} fusion(f32[2,704,1280]{2,1,0:T(8,128)} %copy-done.19, bf16[1280,1280]{1,0:T(8,128)(2,1)} %get-tuple-element.75, f32[2,704,1280]{2,1,0:T(8,128)} %fusion.24), kind=kOutput, calls=%fused_computation.42 | convolution fusion | flops 4626350080 | bytes 21299200 | tf_op jit(solution)/shard_map/cond/branch_1_fun/mti,io->mto/dot_general | solution.py:296
  503.5 6.4 fusion.9
  509.9 13.4 %fusion.13 = bf16[2,704,1280]{2,1,0:T(8,128)(2,1)} fusion(bf16[2,704,1280]{2,1,0:T(8,128)(2,1)} %get-tuple-element.311, f32[2,704]{1,0:T(2,128)S(1)} %broadcast_multiply_fusion, f32[1280]{0:T(1024)S(1)} %copy-done.58, f32[2,704]{1,0:T(2,128)S(1)} %add_rsqrt_fusion.1, bf16[2,704,1280]{2,1,0:T(8,128)(2,1)} %collective-permute-done.17, ...), kind=kLoop, calls=%fused_computation.32 | loop fusion | flops 30638080 | bytes 36077572 | tf_op jit(solution)/shard_map/cond/branch_1_fun/convert_element_type | solution.py:1204
  526.0 20.8 %bitcast_convert_fusion = bf16[1280,1920]{1,0:T(8,128)(2,1)} fusion(bf16[2,1408,1280]{2,1,0:T(8,128)(2,1)} %copy-done.26, bf16[2,1408,1920]{2,1,0:T(8,128)(2,1)} %branch_1_fun.8), kind=kOutput, calls=%fused_computation.20 | convolution fusion | flops 13843660800 | bytes 22937600 | tf_op jit(solution)/shard_map/cond/branch_1_fun/mti,mto->io/dot_general | solution.py:296
  550.9 5.8 add_convert_fusion
  558.1 150.9 %branch_1_fun.9 = (bf16[16,4,16,1280]{3,2,1,0:T(8,128)(2,1)}, f32[8,1280]{1,0:T(8,128)}) custom-call(s32[544]{0:T(1024)} %reshape.603.source_ref, s32[8]{0:T(128)} %get-tuple-element.296.spare_ref, s32[8,1,640]{2,1,0:T(1,128)} %broadcast_in_dim.286.spare_mine_ref, bf16[80,16,1920]{2,1,0:T(8,128)(2,1)} %bitcast.207, bf16[3,80,16,640]{3,2,1,0:T(8,128)(2,1)} %bitcast.191, ...), custom_call_target="tpu_custom_call" | custom-call | bytes 78643200 | tf_op jit(solution)/shard_map/cond/branch_1_fun/pallas_call | solution.py:992
  710.6 15.9 %branch_1_fun.10 = (f32[16,64,1280]{2,1,0:T(8,128)}, f32[16,64,1280]{2,1,0:T(8,128)}, f32[16,64,1280]{2,1,0:T(8,128)}, bf16[16,64,1280]{2,1,0:T(8,128)(2,1)}) custom-call(f32[16]{0:T(128)} %and_select_fusion.4.rate_ref, f32[16,64,1280]{2,1,0:T(8,128)} %get-tuple-element.64.master_ref, f32[16,64,1280]{2,1,0:T(8,128)} %get-tuple-element.79.first_ref, ...), custom_call_target="tpu_custom_call" | custom-call | flops 26214400 | bytes 36700160 | tf_op jit(solution)/shard_map/cond/branch_1_fun/pallas_call | solution.py:1077
  728.3 113.8 %branch_1_fun.11 = (bf16[6,1280,1280]{2,1,0:T(8,128)(2,1)}, f32[8,1280]{1,0:T(8,128)S(1)}) custom-call(s32[480]{0:T(512)S(1)} %copy-done.8, s32[480]{0:T(512)S(1)} %copy-done.6, s32[8]{0:T(128)S(1)} %copy-done.10, s32[8,1,1280]{2,1,0:T(1,128)S(1)} %copy-done.4, bf16[16,64,1280]{2,1,0:T(8,128)(2,1)S(1)} %copy-done.2, f32[8,1280]{1,0:T(8,128)S(1)} %concatenate.63.gain_ref), custom_call_target="tpu_custom_call" | custom-call | bytes 157286400 | tf_op jit(solution)/shard_map/cond/branch_1_fun/pallas_call | solution.py:639
  845.2 16.4 %copy.228 = bf16[6,1280,1280]{2,1,0:T(8,128)(2,1)} copy(bf16[6,1280,1280]{2,1,0:T(8,128)(2,1)} %get-tuple-element.396) | data formatting | bytes 39321600
  (227 shorter events, 96.3 us)
Async XLA Ops:
  14.2 139.8 %collective-permute-start.10 = (bf16[2,704,1280]{2,1,0:T(8,128)(2,1)}, bf16[2,704,1280]{2,1,0:T(8,128)(2,1)}, u32[]{:S(2)}, u32[]{:S(2)}) collective-permute-start(bf16[2,704,1280]{2,1,0:T(8,128)(2,1)} %bitcast.195), channel_id=1, source_target_pairs={{1,2},{2,1},{5,6},{6,5},{9,10},{10,9},{13,14},{14,13},{17,18},{18,... | collective-permute-start | bytes 10813448 | tf_op jit(solution)/shard_map/cond/branch_1_fun/ppermute | solution.py:39
  17.6 140.2 %copy-start.71 = (s32[120]{0:T(128)}, s32[120]{0:T(128)S(1)}, u32[]{:S(2)}) copy-start(s32[120]{0:T(128)S(1)} %convert_reduce_fusion) | copy-start | bytes 1444 | tf_op jit(solution)/shard_map/cond
  21.0 136.8 %copy-start.5 = (s32[480]{0:T(512)}, s32[480]{0:T(512)S(1)}, u32[]{:S(2)}) copy-start(s32[480]{0:T(512)S(1)} %reshape.617.row_ref) | copy-start | bytes 5764 | tf_op jit(solution)/shard_map/cond
  21.1 136.7 %copy-start.7 = (s32[480]{0:T(512)}, s32[480]{0:T(512)S(1)}, u32[]{:S(2)}) copy-start(s32[480]{0:T(512)S(1)} %reshape.615.block_ref) | copy-start | bytes 5764 | tf_op jit(solution)/shard_map/cond
  21.1 132.9 %copy-start.24 = (bf16[2,1,704,1280]{3,2,1,0:T(8,128)(2,1)S(1)}, bf16[2,1,704,1280]{3,2,1,0:T(8,128)(2,1)}, u32[]{:S(2)}) copy-start(bf16[2,1,704,1280]{3,2,1,0:T(8,128)(2,1)} %get-tuple-element.269) | copy-start | bytes 10813444 | tf_op jit(solution)/shard_map/cond
  24.1 137.3 %copy-start.84 = (s32[2,1,44]{2,1,0:T(1,128)S(1)}, s32[2,1,44]{2,1,0:T(1,128)}, u32[]{:S(2)}) copy-start(s32[2,1,44]{2,1,0:T(1,128)} %get-tuple-element.274) | copy-start | bytes 1060 | tf_op jit(solution)/shard_map/cond
  24.2 137.2 %copy-start.85 = (pred[2]{0:T(512)(128)(4,1)}, pred[2]{0:T(512)(128)(4,1)S(1)}, u32[]{:S(2)}) copy-start(pred[2]{0:T(512)(128)(4,1)S(1)} %slice_compare_fusion) | copy-start | bytes 10 | tf_op jit(solution)/shard_map/cond
  25.0 132.8 %copy-start.9 = (s32[8]{0:T(128)}, s32[8]{0:T(128)S(1)}, u32[]{:S(2)}) copy-start(s32[8]{0:T(128)S(1)} %get-tuple-element.295.spare_rank_ref) | copy-start | bytes 100 | tf_op jit(solution)/shard_map/cond
  25.1 128.9 %copy-start.3 = (s32[8,1,1280]{2,1,0:T(1,128)}, s32[8,1,1280]{2,1,0:T(1,128)S(1)}, u32[]{:S(2)}) copy-start(s32[8,1,1280]{2,1,0:T(1,128)S(1)} %broadcast_in_dim.257.spare_mine_ref) | copy-start | bytes 122884 | tf_op jit(solution)/shard_map/cond
  157.8 9.9 %collective-permute-start.12 = (bf16[2,704,1280]{2,1,0:T(8,128)(2,1)}, bf16[2,704,1280]{2,1,0:T(8,128)(2,1)}, u32[]{:S(2)}, u32[]{:S(2)}) collective-permute-start(bf16[2,704,1280]{2,1,0:T(8,128)(2,1)} %get-tuple-element.311), channel_id=1, source_target_pairs={{0,2},{2,0},{1,3},{3,1},{4,6},{6,4},{5,7},{7,5},{8,10},{10,8},{9,1... | collective-permute-start | bytes 10813448 | tf_op jit(solution)/shard_map/cond/branch_1_fun/ppermute | solution.py:51
  161.5 0.7 collective-permute-start.11
  163.8 96.5 %collective-permute-start.15 = (bf16[2,704,1280]{2,1,0:T(8,128)(2,1)}, bf16[2,704,1280]{2,1,0:T(8,128)(2,1)}, u32[]{:S(2)}, u32[]{:S(2)}) collective-permute-start(bf16[2,704,1280]{2,1,0:T(8,128)(2,1)} %bitcast.198), channel_id=1, source_target_pairs={{1,2},{2,1},{5,6},{6,5},{9,10},{10,9},{13,14},{14,13},{17,18},{18,... | collective-permute-start | bytes 10813448 | tf_op jit(solution)/shard_map/cond/branch_1_fun/ppermute | solution.py:39
  257.3 6.7 collective-permute-start.13
  342.6 6.0 collective-permute-start.16
  348.6 105.9 %slice-start.9 = ((s8[4915200]{0:T(1024)(128)(4,1)}), s8[4194304]{0:T(1024)(128)(4,1)S(1)}, s32[]{:S(2)}) async-start(s8[4915200]{0:T(1024)(128)(4,1)} %bitcast.230), calls=%async_computation.14 | async-start | bytes 8388608 | tf_op jit(solution)/shard_map/cond
  480.2 23.2 %collective-permute-start.17 = (bf16[2,704,1280]{2,1,0:T(8,128)(2,1)}, bf16[2,704,1280]{2,1,0:T(8,128)(2,1)}, u32[]{:S(2)}, u32[]{:S(2)}) collective-permute-start(bf16[2,704,1280]{2,1,0:T(8,128)(2,1)} %dynamic-slice_convert_fusion), channel_id=1, source_target_pairs={{0,2},{2,0},{1,3},{3,1},{4,6},{6,4},{5,7},{7,5},{8,10},{10,8},{9,1... | collective-permute-start | bytes 10813448 | tf_op jit(solution)/shard_map/cond/branch_1_fun/ppermute | solution.py:51
  496.6 50.1 %collective-permute-start.14 = (bf16[2,704,1280]{2,1,0:T(8,128)(2,1)}, bf16[2,704,1280]{2,1,0:T(8,128)(2,1)}, u32[]{:S(2)}, u32[]{:S(2)}) collective-permute-start(bf16[2,704,1280]{2,1,0:T(8,128)(2,1)} %add_convert_fusion.1), channel_id=1, source_target_pairs={{1,2},{2,1},{5,6},{6,5},{9,10},{10,9},{13,14},{14,13},{17,18},{18,... | collective-permute-start | bytes 10813448 | tf_op jit(solution)/shard_map/cond/branch_1_fun/ppermute | solution.py:39
  501.9 49.1 %collective-permute-start.19 = (bf16[3,1280,640]{2,1,0:T(8,128)(2,1)}, bf16[3,1280,640]{2,1,0:T(8,128)(2,1)}, u32[]{:S(2)}, u32[]{:S(2)}) collective-permute-start(bf16[3,1280,640]{2,1,0:T(8,128)(2,1)} %constant_dynamic-slice_fusion), channel_id=1, source_target_pairs={{0,2},{2,0},{1,3},{3,1},{4,6},{6,4},{5,7},{7,5},{8,10},{10,8},{9,1... | collective-permute-start | bytes 14745608 | tf_op jit(solution)/shard_map/cond/branch_1_fun/ppermute | solution.py:51
  523.3 319.4 %collective-permute-start.18 = (bf16[2,704,1280]{2,1,0:T(8,128)(2,1)}, bf16[2,704,1280]{2,1,0:T(8,128)(2,1)}, u32[]{:S(2)}, u32[]{:S(2)}) collective-permute-start(bf16[2,704,1280]{2,1,0:T(8,128)(2,1)} %fusion.13), channel_id=1, source_target_pairs={{1,2},{2,1},{5,6},{6,5},{9,10},{10,9},{13,14},{14,13},{17,18},{18,... | collective-permute-start | bytes 10813448 | tf_op jit(solution)/shard_map/cond/branch_1_fun/ppermute | solution.py:39
  556.7 152.3 %copy-start.46 = (f32[2,1280]{1,0:T(2,128)S(1)}, f32[2,1280]{1,0:T(2,128)}, u32[]{:S(2)}) copy-start(f32[2,1280]{1,0:T(2,128)} %get-tuple-element.65) | copy-start | bytes 30724 | tf_op jit(solution)/shard_map/cond
  556.7 152.3 %copy-start.66 = (f32[2,1280]{1,0:T(2,128)S(1)}, f32[2,1280]{1,0:T(2,128)}, u32[]{:S(2)}) copy-start(f32[2,1280]{1,0:T(2,128)} %get-tuple-element.84) | copy-start | bytes 30724 | tf_op jit(solution)/shard_map/cond
  556.7 152.3 %copy-start.68 = (f32[2,1280]{1,0:T(2,128)S(1)}, f32[2,1280]{1,0:T(2,128)}, u32[]{:S(2)}) copy-start(f32[2,1280]{1,0:T(2,128)} %get-tuple-element.86) | copy-start | bytes 30724 | tf_op jit(solution)/shard_map/cond
  556.7 152.3 %copy-start.86 = (pred[2]{0:T(512)(128)(4,1)S(1)}, pred[2]{0:T(512)(128)(4,1)}, u32[]{:S(2)}) copy-start(pred[2]{0:T(512)(128)(4,1)} %copy-done.85) | copy-start | bytes 10 | tf_op jit(solution)/shard_map/cond
  710.6 132.1 %copy-start.23 = (bf16[2,704,1280]{2,1,0:T(8,128)(2,1)S(1)}, bf16[2,704,1280]{2,1,0:T(8,128)(2,1)}, u32[]{:S(2)}) copy-start(bf16[2,704,1280]{2,1,0:T(8,128)(2,1)} %fusion.13) | copy-start | bytes 10813444 | tf_op jit(solution)/shard_map/cond
  (39 other events, 529.9 us)
where the time goes:
time: 883 us; the launch traced here: 869 us
  Pallas kernels  563 us (64%)
  matrix products  138 us (16%)
  other arithmetic  79.3 us (9%)
  local copies, waits for them, and re-layouts  45.4 us (5%)
  starting transfers between devices  19.9 us (2%)
  between operations  14.9 us (2%)
    pallas_call x2, Pallas kernels, gather_pieces(): pl.pallas_call(functools.partial(gather_kernel, split, base // 4 if split...  243 us
    pallas_call x1, Pallas kernels, reduce_slots(): pl.pallas_call(reduce_kernel, in_specs=[smem] * 2 + [vmem, hbm, hbm, vmem...  151 us
    dot_general x12, matrix products, product(): return jnp.einsum(spec, left, right, preferred_element_type=jnp.float32)  138 us
    pallas_call x1, Pallas kernels, attend_back(): pl.pallas_call(attend_back_kernel, grid=(micro, heads), in_specs=[row, ro...  102 us
    pallas_call x1, Pallas kernels, attend(): pl.pallas_call(attend_kernel, grid=(micro, heads), in_specs=[column, colu...  52.2 us
  transfers between devices with their start and end apart: 10, of which 2 were waited for; matrix products, arithmetic and copies ran while one was open for 14% of the time, Pallas kernels for 53%

commit v1 on v0

--- a/solution.py
+++ b/solution.py
@@ -114,13 +114,14 @@
     window, mine = head_window(head, q_ref.shape[2])
     stat_lane = lax.broadcasted_iota(jnp.int32, (1, LANES), 1)
     values = jnp.where(mine, v_ref[0, :, window], 1)
+    keys_side = k_ref[0, :, window].T
     for first, count, parts in query_blocks(q_ref.shape[1]):
         rows = pl.ds(first, count)
         query = scaled_query(q_ref[0, rows, window], mine)
         scores = []
         for key_first, keys, kind in parts:
-            raw = lax.dot_general(
-                query, k_ref[0, pl.ds(key_first, keys), window], NT, preferred_element_type=jnp.float32
+            raw = jnp.dot(
+                query, keys_side[:, key_first : key_first + keys], preferred_element_type=jnp.float32
             )
             if kind != "all":
                 ok = allowed_pairs(
@@ -192,24 +193,40 @@
         dk_sum[...] = jnp.zeros_like(dk_sum)
         dv_sum[...] = jnp.zeros_like(dv_sum)
 
-    ones = jnp.ones((8, WINDOW), jnp.float32)
+    lane = lax.broadcasted_iota(jnp.int32, (1, WINDOW), 1)
+    after = (head + 1) * HEAD - window.start
+    spots = [lane == lax.rem(after + i, WINDOW) for i in range(3)]
+    stat_lane = lax.broadcasted_iota(jnp.int32, (1, LANES), 1)
+    keys_all = jnp.where(spots[0] | spots[1] | spots[2], 1, k_ref[0, :, window])
+    values_all = jnp.where(spots[0] | spots[1], 1, v_ref[0, :, window])
+
+    def less(rows, column, count):
+        rest = column
+        for spot in spots[:count]:
+            piece = rest.astype(jnp.bfloat16).astype(jnp.float32)
+            rows = jnp.where(spot, -piece, rows)
+            rest = rest - piece
+        return rows.astype(jnp.bfloat16)
+
     for first, count, parts in query_blocks(q_ref.shape[1]):
         rows = pl.ds(first, count)
-        query = jnp.where(mine, q_ref[0, rows, window], 0)
-        scaled = scaled_query(q_ref[0, rows, window], mine)
+        raw_query = q_ref[0, rows, window]
+        query = jnp.where(mine, raw_query, 0)
         grad = jnp.where(mine, g_ref[0, rows, window], 0)
-        lse = lse_ref[0, pl.ds(head, 1), rows]
-        gains = grad.astype(jnp.float32) * a_ref[0, rows, window].astype(jnp.float32)
-        row_total = lax.dot_general(
-            ones, gains, NT, precision=lax.Precision.HIGHEST, preferred_element_type=jnp.float32
-        )[0:1]
+        wide_grad = grad.astype(jnp.float32)
+        lse = jnp.sum(jnp.where(stat_lane == head, lse_ref[0, rows, :], 0.0), axis=1, keepdims=True)
+        row_total = jnp.sum(
+            wide_grad * a_ref[0, rows, window].astype(jnp.float32), axis=1, keepdims=True
+        )
+        query_less = less(scaled_query(raw_query, mine).astype(jnp.float32), lse, 3)
+        grad_less = less(wide_grad, row_total, 2)
         grad_query = 0.0
         for key_first, keys, kind in parts:
             where = pl.ds(key_first, keys)
-            raw = lax.dot_general(
-                k_ref[0, where, window], scaled, NT, preferred_element_type=jnp.float32
+            part = slice(key_first, key_first + keys)
+            prob = jnp.exp2(
+                lax.dot_general(keys_all[part], query_less, NT, preferred_element_type=jnp.float32)
             )
-            prob = jnp.exp2(raw - lse)
             if kind != "all":
                 ok = allowed_pairs(
                     kind,
@@ -221,15 +238,15 @@
                 )
                 prob = jnp.where(ok, prob, 0.0)
             grad_prob = lax.dot_general(
-                v_ref[0, where, window], grad, NT, preferred_element_type=jnp.float32
+                values_all[part], grad_less, NT, preferred_element_type=jnp.float32
             )
-            grad_raw = (prob * (grad_prob - row_total)).astype(jnp.bfloat16)
+            grad_raw = (prob * grad_prob).astype(jnp.bfloat16)
             dv_sum[where, window] += jnp.dot(
                 prob.astype(jnp.bfloat16), grad, preferred_element_type=jnp.float32
             )
             dk_sum[where, window] += jnp.dot(grad_raw, query, preferred_element_type=jnp.float32)
             grad_query = grad_query + lax.dot_general(
-                grad_raw, k_ref[0, where, window], TN, preferred_element_type=jnp.float32
+                grad_raw, keys_all[part], TN, preferred_element_type=jnp.float32
             )
         out_ref[0, rows, window] = jnp.where(
             mine, (grad_query * SCALE).astype(jnp.bfloat16), out_ref[0, rows, window]
@@ -257,7 +274,7 @@
         in_specs=[
             row,
             row,
-            pl.BlockSpec((1, heads, length), lambda m, h: (m, 0, 0)),
+            pl.BlockSpec((1, length, LANES), lambda m, h: (m, 0, 0)),
             part(0),
             part(1),
             part(2),
@@ -1154,7 +1171,6 @@
     normed_one = lax.optimization_barrier(normed_one)
     qkv = product(normed_one, qkv_weight, "mtd,de->mte").astype(jnp.bfloat16)
     attended_half, lse = attend(qkv, limit, branch)
-    lse_rows = jnp.transpose(lse[:, :, : half // HEAD], (0, 2, 1))
     attended = by_core(
         mine(attended_half, 1, rows, core), partner(mine(attended_half, 1, rows, 1 - core)), 2
     )
@@ -1189,13 +1205,13 @@
     grad_half = by_core(
         mine(grad_attended, 2, half, core), partner(mine(grad_attended, 2, half, 1 - core)), 1
     )
-    grad_qkv_rows = attend_back(qkv, grad_half, attended_half, lse_rows, limit, branch)
+    grad_qkv_rows = attend_back(qkv, grad_half, attended_half, lse, limit, branch)
     grad_qkv = product(normed_one, grad_qkv_rows, "mti,mto->io")
     early = grad_qkv.astype(jnp.bfloat16)
 
-    grad_normed_part = product(grad_qkv_rows, qkv_weight, "mte,de->mtd")
-    grad_normed_one = mine(grad_normed_part, 1, rows, core) + partner(
-        mine(grad_normed_part, 1, rows, 1 - core).astype(jnp.bfloat16)
+    grad_normed_part = product(grad_qkv_rows, qkv_weight, "mte,de->mtd").astype(jnp.bfloat16)
+    grad_normed_one = mine(grad_normed_part, 1, rows, core).astype(jnp.float32) + partner(
+        mine(grad_normed_part, 1, rows, 1 - core)
     ).astype(jnp.float32)
     unit_one, scale_one = unit(residual)
     gain_one_grad = jnp.sum(grad_normed_one * unit_one, axis=(0, 1))

time: 883 us -> 848 us (0.960)
  Pallas kernels: 563 us -> 548 us
    pallas_call x1, Pallas kernels: 102 us -> 88.5 us  [attend_back(): pl.pallas_call(attend_back_kernel, grid=(micro, heads), in_specs=[row, ro...]
  transfers between devices with their start and end apart: 10 -> 10, of which waited for: 2 -> 3; matrix products, arithmetic and copies ran while one was open for 14% -> 13% of each run, Pallas kernels for 53% -> 55%
where the time goes in v1:
time: 848 us; the launch traced here: 843 us
  Pallas kernels  548 us (65%)
  matrix products  132 us (16%)
  other arithmetic  75.7 us (9%)
  local copies, waits for them, and re-layouts  42.1 us (5%)
  starting transfers between devices  19.6 us (2%)
  between operations  15.2 us (2%)
    pallas_call x2, Pallas kernels, gather_pieces(): pl.pallas_call(functools.partial(gather_kernel, split, base // 4 if split...  239 us
    pallas_call x1, Pallas kernels, reduce_slots(): pl.pallas_call(reduce_kernel, in_specs=[smem] * 2 + [vmem, hbm, hbm, vmem...  151 us
    dot_general x12, matrix products, product(): return jnp.einsum(spec, left, right, preferred_element_type=jnp.float32)  132 us
    pallas_call x1, Pallas kernels, attend_back(): pl.pallas_call(attend_back_kernel, grid=(micro, heads), in_specs=[row, ro...  88.5 us
    pallas_call x1, Pallas kernels, attend(): pl.pallas_call(attend_kernel, grid=(micro, heads), in_specs=[column, colu...  53.6 us
  transfers between devices with their start and end apart: 10, of which 3 were waited for; matrix products, arithmetic and copies ran while one was open for 13% of the time, Pallas kernels for 55%

profile of v1, /device:TPU:0, one launch (start us, length us, event | category | flops | bytes accessed | tf_op | source)
XLA Modules:
  0.0 842.5 jit_solution(6193583379246383533)
XLA Ops:
  9.4 809.3 %conditional.1 = (f32[16,64,1280]{2,1,0:T(8,128)}, f32[16,64,1280]{2,1,0:T(8,128)}, f32[16,64,1280]{2,1,0:T(8,128)}, bf16[2,1,704,1280]{3,2,0,1:T(8,128)(2,1)}, ...) conditional(s32[]{:T(128)} %bitcast.65, ...), branch_computations={%region_2.17_spmd, %region_17.38_spmd} | conditional | flops 164633149440 | bytes 1624319232 | solution.py:1115
  25.5 128.8 %branch_1_fun.6 = (bf16[1280,1920]{1,0:T(8,128)(2,1)}, bf16[1280,1280]{1,0:T(8,128)(2,1)S(1)}, bf16[1280,1280]{1,0:T(8,128)(2,1)}, bf16[1280,1280]{1,0:T(8,128)(2,1)}, f32[8,1280]{1,0:T(8,128)S(1)}) custom-call(s32[480]{0:T(512)S(1)} %reshape.615.block_ref, s32[480]{0:T(512)S(1)} %reshape.617.row_ref, s32[8]{0:T(128)S(1)} %get-tuple-element.295.spare_rank_ref, ...), custom_call_target="tpu_custom_call" | custom-call | bytes 157286400 | tf_op jit(solution)/shard_map/cond/branch_1_fun/pallas_call | solution.py:656
  168.0 7.1 fusion
  175.1 6.9 fusion.2
  185.0 17.1 %convolution_convert_fusion.1.q_ref.k_ref.v_ref = bf16[2,1408,1920]{2,1,0:T(8,128)(2,1)} fusion(bf16[2,1408,1280]{2,1,0:T(8,128)(2,1)S(1)} %fusion.2, bf16[1280,1920]{1,0:T(8,128)(2,1)S(1)} %bitcast.225), kind=kOutput, calls=%fused_computation.16 | convolution fusion | flops 13846609920 | bytes 22937600 | tf_op jit(solution)/shard_map/cond/branch_1_fun/mtd,de->mte/dot_general | solution.py:313
  202.1 53.6 %branch_1_fun.7 = (bf16[2,1408,640]{2,1,0:T(8,128)(2,1)S(1)}, f32[2,1408,128]{2,1,0:T(8,128)S(1)}) custom-call(s32[2,384,1]{2,1,0:T(8,128)S(1)} %reshape.697.limit_ref, s32[2,384,1]{2,1,0:T(8,128)S(1)} %reshape.698.branch_ref, bf16[2,1408,1920]{2,1,0:T(8,128)(2,1)} %convolution_convert_fusion.1.q_ref.k_ref.v_ref, ...), custom_call_target="tpu_custom_call" | custom-call | flops 24360517632 | bytes 14417920 | tf_op jit(solution)/shard_map/cond/branch_1_fun/pallas_call | solution.py:163
  266.4 8.8 %multiply_reduce_fusion.2 = (f32[2,704]{1,0:T(2,128)S(1)}, f32[2,704,1280]{2,1,0:T(8,128)S(1)}) fusion(bf16[1280,1280]{1,0:T(8,128)(2,1)S(1)} %copy-done.12, bf16[2,704,640]{2,1,0:T(8,128)(2,1)} %collective-permute-done.13, bf16[2,704,640]{2,1,0:T(8,128)(2,1)S(1)} %copy-done.39, pred[]{:T(512)S(6)} %eq.149, bf16[2,704,1280]{2,1,0:T(8,128)(2,1)} %get-tuple-element.311), kind=kOutput, calls=%fused_computation.46 | convolution fusion | flops 4637161984 | bytes 17700352 | tf_op jit(solution)/shard_map/cond/branch_1_fun/mti,io->mto/dot_general | solution.py:313
  275.2 7.3 fusion.24
  282.4 9.6 %fusion.17 = bf16[1,1280,1280]{2,1,0:T(8,128)(2,1)} fusion(bf16[2,704,1280]{2,1,0:T(8,128)(2,1)S(1)} %broadcast_select_fusion, f32[2,704,1280]{2,1,0:T(8,128)} %fusion.24), kind=kOutput, calls=%fused_computation.48 | convolution fusion | flops 4624384000 | bytes 14090240 | tf_op jit(solution)/shard_map/cond/branch_1_fun/mti,mto->io/dot_general | solution.py:313
  292.0 8.1 multiply_convert_fusion
  302.0 7.6 fusion.18
  309.5 9.0 %multiply_reduce_fusion = (f32[1280]{0:T(1024)S(1)}, f32[2,704]{1,0:T(2,128)S(1)}, f32[2,704,1280]{2,1,0:T(8,128)S(1)}) fusion(f32[2,704,1280]{2,1,0:T(8,128)S(1)} %get-tuple-element.338, f32[2,704]{1,0:T(2,128)S(1)} %add_rsqrt_fusion.2, f32[1280]{0:T(1024)S(1)} %get-tuple-element.293, bf16[2,704,1280]{2,1,0:T(8,128)(2,1)} %copy-done.102, ...), kind=kOutput, calls=%fused_computation.37 | convolution fusion | flops 4624545280 | bytes 21320704 | tf_op jit(solution)/shard_map/cond/branch_1_fun/mto,io->mti/dot_general | solution.py:313
  322.6 8.7 %fusion.19 = bf16[1,1280,1280]{2,1,0:T(8,128)(2,1)S(1)} fusion(bf16[2,704,1280]{2,1,0:T(8,128)(2,1)} %fusion.48, bf16[2,704,640]{2,1,0:T(8,128)(2,1)} %collective-permute-done.13, bf16[2,704,640]{2,1,0:T(8,128)(2,1)S(1)} %copy-done.39, pred[]{:T(512)S(6)} %eq.149), kind=kOutput, calls=%fused_computation.50 | convolution fusion | flops 4631592960 | bytes 10485761 | tf_op jit(solution)/shard_map/cond/branch_1_fun/mti,mto->io/dot_general | solution.py:313
  336.1 5.2 convolution_convert_fusion.2
  351.4 88.5 %branch_1_fun.8 = bf16[2,1408,1920]{2,1,0:T(8,128)(2,1)} custom-call(s32[2,1,384]{2,1,0:T(1,128)} %reshape.695.limit_ref, s32[2,1,384]{2,1,0:T(1,128)} %reshape.696.branch_ref, f32[2,1408,128]{2,1,0:T(8,128)} %copy-done.13, bf16[2,1408,1920]{2,1,0:T(8,128)(2,1)} %convolution_convert_fusion.1.q_ref.k_ref.v_ref, ...), custom_call_target="tpu_custom_call" | custom-call | flops 56841207808 | bytes 25231360 | tf_op jit(solution)/shard_map/cond/branch_1_fun/pallas_call | solution.py:271
  439.9 17.7 %convolution_convert_fusion = bf16[2,1408,1280]{2,1,0:T(8,128)(2,1)S(1)} fusion(bf16[2,1408,1920]{2,1,0:T(8,128)(2,1)} %branch_1_fun.8, bf16[1280,1920]{1,0:T(8,128)(2,1)S(1)} %bitcast.227), kind=kOutput, calls=%fused_computation.15 | convolution fusion | flops 13844807680 | bytes 22937600 | tf_op jit(solution)/shard_map/cond/branch_1_fun/mte,de->mtd/dot_general | solution.py:313
  465.6 12.0 %add_convert_fusion.1 = bf16[2,704,1280]{2,1,0:T(8,128)(2,1)S(1)} fusion(f32[2,704,1280]{2,1,0:T(8,128)} %copy-done.21, bf16[1280,1280]{1,0:T(8,128)(2,1)} %get-tuple-element.75, f32[2,704,1280]{2,1,0:T(8,128)} %fusion.24), kind=kOutput, calls=%fused_computation.42 | convolution fusion | flops 4626350080 | bytes 21299200 | tf_op jit(solution)/shard_map/cond/branch_1_fun/mti,io->mto/dot_general | solution.py:313
  489.2 12.3 %fusion.13 = bf16[2,704,1280]{2,1,0:T(8,128)(2,1)} fusion(bf16[2,704,1280]{2,1,0:T(8,128)(2,1)} %get-tuple-element.311, bf16[2,704,1280]{2,1,0:T(8,128)(2,1)} %collective-permute-done.17, f32[2,704]{1,0:T(2,128)S(1)} %broadcast_multiply_fusion, f32[1280]{0:T(1024)S(1)} %copy-done.61, f32[2,704]{1,0:T(2,128)S(1)} %add_rsqrt_fusion.1, ...), kind=kLoop, calls=%fused_computation.33 | loop fusion | flops 32440320 | bytes 32473092 | tf_op jit(solution)/shard_map/cond/branch_1_fun/convert_element_type | solution.py:1220
  503.9 20.9 %bitcast_convert_fusion = bf16[1280,1920]{1,0:T(8,128)(2,1)} fusion(bf16[2,1408,1280]{2,1,0:T(8,128)(2,1)} %copy-done.29, bf16[2,1408,1920]{2,1,0:T(8,128)(2,1)} %branch_1_fun.8), kind=kOutput, calls=%fused_computation.21 | convolution fusion | flops 13843660800 | bytes 22937600 | tf_op jit(solution)/shard_map/cond/branch_1_fun/mti,mto->io/dot_general | solution.py:313
  527.1 5.8 add_convert_fusion
  534.3 151.1 %branch_1_fun.9 = (bf16[16,4,16,1280]{3,2,1,0:T(8,128)(2,1)}, f32[8,1280]{1,0:T(8,128)}) custom-call(s32[544]{0:T(1024)} %reshape.603.source_ref, s32[8]{0:T(128)} %get-tuple-element.296.spare_ref, s32[8,1,640]{2,1,0:T(1,128)} %broadcast_in_dim.286.spare_mine_ref, bf16[80,16,1920]{2,1,0:T(8,128)(2,1)} %bitcast.203, bf16[3,80,16,640]{3,2,1,0:T(8,128)(2,1)} %bitcast.187, ...), custom_call_target="tpu_custom_call" | custom-call | bytes 78643200 | tf_op jit(solution)/shard_map/cond/branch_1_fun/pallas_call | solution.py:1009
  686.4 15.6 %branch_1_fun.10 = (f32[16,64,1280]{2,1,0:T(8,128)}, f32[16,64,1280]{2,1,0:T(8,128)}, f32[16,64,1280]{2,1,0:T(8,128)}, bf16[16,64,1280]{2,1,0:T(8,128)(2,1)}) custom-call(f32[16]{0:T(128)} %and_select_fusion.4.rate_ref, f32[16,64,1280]{2,1,0:T(8,128)} %get-tuple-element.64.master_ref, f32[16,64,1280]{2,1,0:T(8,128)} %get-tuple-element.79.first_ref, ...), custom_call_target="tpu_custom_call" | custom-call | flops 26214400 | bytes 36700160 | tf_op jit(solution)/shard_map/cond/branch_1_fun/pallas_call | solution.py:1094
  703.8 110.4 %branch_1_fun.11 = (bf16[6,1280,1280]{2,1,0:T(8,128)(2,1)}, f32[8,1280]{1,0:T(8,128)S(1)}) custom-call(s32[480]{0:T(512)S(1)} %copy-done.8, s32[480]{0:T(512)S(1)} %copy-done.6, s32[8]{0:T(128)S(1)} %copy-done.10, s32[8,1,1280]{2,1,0:T(1,128)S(1)} %copy-done.4, bf16[16,64,1280]{2,1,0:T(8,128)(2,1)S(1)} %copy-done.2, f32[8,1280]{1,0:T(8,128)S(1)} %concatenate.63.gain_ref), custom_call_target="tpu_custom_call" | custom-call | bytes 157286400 | tf_op jit(solution)/shard_map/cond/branch_1_fun/pallas_call | solution.py:656
  818.8 16.4 %copy.216 = bf16[6,1280,1280]{2,1,0:T(8,128)(2,1)} copy(bf16[6,1280,1280]{2,1,0:T(8,128)(2,1)} %get-tuple-element.396) | data formatting | bytes 39321600
  (241 shorter events, 92.5 us)
Async XLA Ops:
  14.6 139.7 %collective-permute-start.10 = (bf16[2,704,1280]{2,1,0:T(8,128)(2,1)}, bf16[2,704,1280]{2,1,0:T(8,128)(2,1)}, u32[]{:S(2)}, u32[]{:S(2)}) collective-permute-start(bf16[2,704,1280]{2,1,0:T(8,128)(2,1)} %bitcast.191), channel_id=1, source_target_pairs={{1,2},{2,1},{5,6},{6,5},{9,10},{10,9},{13,14},{14,13},{17,18},{18,... | collective-permute-start | bytes 10813448 | tf_op jit(solution)/shard_map/cond/branch_1_fun/ppermute | solution.py:39
  18.0 140.1 %copy-start.74 = (s32[120]{0:T(128)}, s32[120]{0:T(128)S(1)}, u32[]{:S(2)}) copy-start(s32[120]{0:T(128)S(1)} %convert_reduce_fusion) | copy-start | bytes 1444 | tf_op jit(solution)/shard_map/cond
  21.3 136.8 %copy-start.5 = (s32[480]{0:T(512)}, s32[480]{0:T(512)S(1)}, u32[]{:S(2)}) copy-start(s32[480]{0:T(512)S(1)} %reshape.617.row_ref) | copy-start | bytes 5764 | tf_op jit(solution)/shard_map/cond
  21.4 136.7 %copy-start.7 = (s32[480]{0:T(512)}, s32[480]{0:T(512)S(1)}, u32[]{:S(2)}) copy-start(s32[480]{0:T(512)S(1)} %reshape.615.block_ref) | copy-start | bytes 5764 | tf_op jit(solution)/shard_map/cond
  21.4 133.0 %copy-start.27 = (bf16[2,1,704,1280]{3,2,1,0:T(8,128)(2,1)S(1)}, bf16[2,1,704,1280]{3,2,1,0:T(8,128)(2,1)}, u32[]{:S(2)}) copy-start(bf16[2,1,704,1280]{3,2,1,0:T(8,128)(2,1)} %get-tuple-element.269) | copy-start | bytes 10813444 | tf_op jit(solution)/shard_map/cond
  24.4 137.3 %copy-start.91 = (s32[2,1,44]{2,1,0:T(1,128)S(1)}, s32[2,1,44]{2,1,0:T(1,128)}, u32[]{:S(2)}) copy-start(s32[2,1,44]{2,1,0:T(1,128)} %get-tuple-element.274) | copy-start | bytes 1060 | tf_op jit(solution)/shard_map/cond
  24.5 137.2 %copy-start.92 = (pred[2]{0:T(512)(128)(4,1)}, pred[2]{0:T(512)(128)(4,1)S(1)}, u32[]{:S(2)}) copy-start(pred[2]{0:T(512)(128)(4,1)S(1)} %slice_compare_fusion) | copy-start | bytes 10 | tf_op jit(solution)/shard_map/cond
  25.4 132.7 %copy-start.9 = (s32[8]{0:T(128)}, s32[8]{0:T(128)S(1)}, u32[]{:S(2)}) copy-start(s32[8]{0:T(128)S(1)} %get-tuple-element.295.spare_rank_ref) | copy-start | bytes 100 | tf_op jit(solution)/shard_map/cond
  25.4 128.9 %copy-start.3 = (s32[8,1,1280]{2,1,0:T(1,128)}, s32[8,1,1280]{2,1,0:T(1,128)S(1)}, u32[]{:S(2)}) copy-start(s32[8,1,1280]{2,1,0:T(1,128)S(1)} %broadcast_in_dim.257.spare_mine_ref) | copy-start | bytes 122884 | tf_op jit(solution)/shard_map/cond
  158.1 9.9 %collective-permute-start.12 = (bf16[2,704,1280]{2,1,0:T(8,128)(2,1)}, bf16[2,704,1280]{2,1,0:T(8,128)(2,1)}, u32[]{:S(2)}, u32[]{:S(2)}) collective-permute-start(bf16[2,704,1280]{2,1,0:T(8,128)(2,1)} %get-tuple-element.311), channel_id=1, source_target_pairs={{0,2},{2,0},{1,3},{3,1},{4,6},{6,4},{5,7},{7,5},{8,10},{10,8},{9,1... | collective-permute-start | bytes 10813448 | tf_op jit(solution)/shard_map/cond/branch_1_fun/ppermute | solution.py:51
  161.8 0.7 collective-permute-start.11
  164.3 98.4 %collective-permute-start.15 = (bf16[2,704,1280]{2,1,0:T(8,128)(2,1)}, bf16[2,704,1280]{2,1,0:T(8,128)(2,1)}, u32[]{:S(2)}, u32[]{:S(2)}) collective-permute-start(bf16[2,704,1280]{2,1,0:T(8,128)(2,1)} %bitcast.194), channel_id=1, source_target_pairs={{1,2},{2,1},{5,6},{6,5},{9,10},{10,9},{13,14},{14,13},{17,18},{18,... | collective-permute-start | bytes 10813448 | tf_op jit(solution)/shard_map/cond/branch_1_fun/ppermute | solution.py:39
  259.7 6.7 collective-permute-start.13
  343.0 4.2 collective-permute-start.16
  347.1 92.8 %slice-start.9 = ((s8[4915200]{0:T(1024)(128)(4,1)}), s8[4194304]{0:T(1024)(128)(4,1)S(1)}, s32[]{:S(2)}) async-start(s8[4915200]{0:T(1024)(128)(4,1)} %bitcast.226), calls=%async_computation.14 | async-start | bytes 8388608 | tf_op jit(solution)/shard_map/cond
  351.4 88.5 %slice-start.10 = ((s8[4915200]{0:T(1024)(128)(4,1)}), s8[720896]{0:T(1024)(128)(4,1)S(1)}, s32[]{:S(2)}) async-start(s8[4915200]{0:T(1024)(128)(4,1)} %bitcast.226), calls=%async_computation.15 | async-start | bytes 1441792 | tf_op jit(solution)/shard_map/cond
  462.8 21.7 %collective-permute-start.17 = (bf16[2,704,1280]{2,1,0:T(8,128)(2,1)}, bf16[2,704,1280]{2,1,0:T(8,128)(2,1)}, u32[]{:S(2)}, u32[]{:S(2)}) collective-permute-start(bf16[2,704,1280]{2,1,0:T(8,128)(2,1)} %constant_dynamic-slice_fusion.1), channel_id=1, source_target_pairs={{0,2},{2,0},{1,3},{3,1},{4,6},{6,4},{5,7},{7,5},{8,10},{10,8},{9,1... | collective-permute-start | bytes 10813448 | tf_op jit(solution)/shard_map/cond/branch_1_fun/ppermute | solution.py:51
  477.7 47.2 %collective-permute-start.14 = (bf16[2,704,1280]{2,1,0:T(8,128)(2,1)S(1)}, bf16[2,704,1280]{2,1,0:T(8,128)(2,1)}, u32[]{:S(2)}, u32[]{:S(2)}) collective-permute-start(bf16[2,704,1280]{2,1,0:T(8,128)(2,1)S(1)} %add_convert_fusion.1), channel_id=1, source_target_pairs={{1,2},{2,1},{5,6},{6,5},{9,10},{10,9},{13,14},{14,13},{17,18},{18,... | collective-permute-start | bytes 10813448 | tf_op jit(solution)/shard_map/cond/branch_1_fun/ppermute | solution.py:39
  483.0 44.1 %collective-permute-start.19 = (bf16[3,1280,640]{2,1,0:T(8,128)(2,1)}, bf16[3,1280,640]{2,1,0:T(8,128)(2,1)}, u32[]{:S(2)}, u32[]{:S(2)}) collective-permute-start(bf16[3,1280,640]{2,1,0:T(8,128)(2,1)} %constant_dynamic-slice_fusion), channel_id=1, source_target_pairs={{0,2},{2,0},{1,3},{3,1},{4,6},{6,4},{5,7},{7,5},{8,10},{10,8},{9,1... | collective-permute-start | bytes 14745608 | tf_op jit(solution)/shard_map/cond/branch_1_fun/ppermute | solution.py:51
  501.5 312.7 %collective-permute-start.18 = (bf16[2,704,1280]{2,1,0:T(8,128)(2,1)}, bf16[2,704,1280]{2,1,0:T(8,128)(2,1)}, u32[]{:S(2)}, u32[]{:S(2)}) collective-permute-start(bf16[2,704,1280]{2,1,0:T(8,128)(2,1)} %fusion.13), channel_id=1, source_target_pairs={{1,2},{2,1},{5,6},{6,5},{9,10},{10,9},{13,14},{14,13},{17,18},{18,... | collective-permute-start | bytes 10813448 | tf_op jit(solution)/shard_map/cond/branch_1_fun/ppermute | solution.py:39
  532.9 152.5 %copy-start.49 = (f32[2,1280]{1,0:T(2,128)S(1)}, f32[2,1280]{1,0:T(2,128)}, u32[]{:S(2)}) copy-start(f32[2,1280]{1,0:T(2,128)} %get-tuple-element.65) | copy-start | bytes 30724 | tf_op jit(solution)/shard_map/cond
  532.9 152.5 %copy-start.69 = (f32[2,1280]{1,0:T(2,128)S(1)}, f32[2,1280]{1,0:T(2,128)}, u32[]{:S(2)}) copy-start(f32[2,1280]{1,0:T(2,128)} %get-tuple-element.84) | copy-start | bytes 30724 | tf_op jit(solution)/shard_map/cond
  532.9 152.5 %copy-start.71 = (f32[2,1280]{1,0:T(2,128)S(1)}, f32[2,1280]{1,0:T(2,128)}, u32[]{:S(2)}) copy-start(f32[2,1280]{1,0:T(2,128)} %get-tuple-element.86) | copy-start | bytes 30724 | tf_op jit(solution)/shard_map/cond
  532.9 152.5 %copy-start.93 = (pred[2]{0:T(512)(128)(4,1)S(1)}, pred[2]{0:T(512)(128)(4,1)}, u32[]{:S(2)}) copy-start(pred[2]{0:T(512)(128)(4,1)} %copy-done.92) | copy-start | bytes 10 | tf_op jit(solution)/shard_map/cond
  (47 other events, 481.4 us)

commit v2 on v1

--- a/solution.py
+++ b/solution.py
@@ -16,6 +16,7 @@
 LANES = 128
 WINDOW = 256
 QUERY_BLOCK = 256
+KEY_BLOCK = 512
 
 NORM_EPS = 1e-06
 BETA_ONE = 0.5
@@ -115,9 +116,9 @@
     stat_lane = lax.broadcasted_iota(jnp.int32, (1, LANES), 1)
     values = jnp.where(mine, v_ref[0, :, window], 1)
     keys_side = k_ref[0, :, window].T
-    for first, count, parts in query_blocks(q_ref.shape[1]):
-        rows = pl.ds(first, count)
-        query = scaled_query(q_ref[0, rows, window], mine)
+
+    def score(first, count, parts):
+        query = scaled_query(q_ref[0, pl.ds(first, count), window], mine)
         scores = []
         for key_first, keys, kind in parts:
             raw = jnp.dot(
@@ -134,6 +135,10 @@
                 )
                 raw = jnp.where(ok, raw, MASKED)
             scores.append(raw)
+        return scores
+
+    def weigh(scores, first, count, parts):
+        rows = pl.ds(first, count)
         top = functools.reduce(jnp.maximum, [jnp.max(s, axis=1, keepdims=True) for s in scores])
         gained = 0.0
         for raw, (key_first, keys, kind) in zip(scores, parts):
@@ -148,6 +153,13 @@
         lse_ref[0, rows, :] = jnp.where(
             stat_lane == head, top + jnp.log2(weight_sum), lse_ref[0, rows, :]
         )
+
+    blocks = query_blocks(q_ref.shape[1])
+    scores = score(*blocks[0])
+    for block, following in zip(blocks, blocks[1:] + [None]):
+        later = score(*following) if following else None
+        weigh(scores, *block)
+        scores = later
 
 
 def attend(qkv, limit, branch):
@@ -208,7 +220,7 @@
             rest = rest - piece
         return rows.astype(jnp.bfloat16)
 
-    for first, count, parts in query_blocks(q_ref.shape[1]):
+    def factors(first, count):
         rows = pl.ds(first, count)
         raw_query = q_ref[0, rows, window]
         query = jnp.where(mine, raw_query, 0)
@@ -219,38 +231,60 @@
             wide_grad * a_ref[0, rows, window].astype(jnp.float32), axis=1, keepdims=True
         )
         query_less = less(scaled_query(raw_query, mine).astype(jnp.float32), lse, 3)
-        grad_less = less(wide_grad, row_total, 2)
-        grad_query = 0.0
+        return (query, grad, query_less, less(wide_grad, row_total, 2))
+
+    def scores(part, block):
+        query, grad, query_less, grad_less = block
+        return (
+            lax.dot_general(keys_all[part], query_less, NT, preferred_element_type=jnp.float32),
+            lax.dot_general(values_all[part], grad_less, NT, preferred_element_type=jnp.float32),
+        )
+
+    def spread(found, part, kind, block):
+        query, grad, query_less, grad_less = block
+        raw, grad_prob = found
+        prob = jnp.exp2(raw)
+        if kind != "all":
+            ok = allowed_pairs(
+                kind,
+                part.start,
+                lax.broadcasted_iota(jnp.int32, raw.shape, 0),
+                lax.broadcasted_iota(jnp.int32, raw.shape, 1),
+                limit_ref[0],
+                branch_ref[0],
+            )
+            prob = jnp.where(ok, prob, 0.0)
+        grad_raw = (prob * grad_prob).astype(jnp.bfloat16)
+        dv_sum[part, window] += jnp.dot(
+            prob.astype(jnp.bfloat16), grad, preferred_element_type=jnp.float32
+        )
+        dk_sum[part, window] += jnp.dot(grad_raw, query, preferred_element_type=jnp.float32)
+        return lax.dot_general(grad_raw, keys_all[part], TN, preferred_element_type=jnp.float32)
+
+    units = []
+    for first, count, parts in query_blocks(q_ref.shape[1]):
         for key_first, keys, kind in parts:
-            where = pl.ds(key_first, keys)
-            part = slice(key_first, key_first + keys)
-            prob = jnp.exp2(
-                lax.dot_general(keys_all[part], query_less, NT, preferred_element_type=jnp.float32)
+            for cut in range(key_first, key_first + keys, KEY_BLOCK):
+                part = slice(cut, min(cut + KEY_BLOCK, key_first + keys))
+                units.append((first, count, part, kind))
+    block = factors(*units[0][:2])
+    found = scores(units[0][2], block)
+    grad_query = 0.0
+    for unit, following in zip(units, units[1:] + [None]):
+        first, count, part, kind = unit
+        same = following and following[0] == first
+        if following:
+            later_block = block if same else factors(*following[:2])
+            later = scores(following[2], later_block)
+        grad_query = grad_query + spread(found, part, kind, block)
+        if not same:
+            rows = pl.ds(first, count)
+            out_ref[0, rows, window] = jnp.where(
+                mine, (grad_query * SCALE).astype(jnp.bfloat16), out_ref[0, rows, window]
             )
-            if kind != "all":
-                ok = allowed_pairs(
-                    kind,
-                    key_first,
-                    lax.broadcasted_iota(jnp.int32, (keys, count), 0),
-                    lax.broadcasted_iota(jnp.int32, (keys, count), 1),
-                    limit_ref[0],
-                    branch_ref[0],
-                )
-                prob = jnp.where(ok, prob, 0.0)
-            grad_prob = lax.dot_general(
-                values_all[part], grad_less, NT, preferred_element_type=jnp.float32
-            )
-            grad_raw = (prob * grad_prob).astype(jnp.bfloat16)
-            dv_sum[where, window] += jnp.dot(
-                prob.astype(jnp.bfloat16), grad, preferred_element_type=jnp.float32
-            )
-            dk_sum[where, window] += jnp.dot(grad_raw, query, preferred_element_type=jnp.float32)
-            grad_query = grad_query + lax.dot_general(
-                grad_raw, keys_all[part], TN, preferred_element_type=jnp.float32
-            )
-        out_ref[0, rows, window] = jnp.where(
-            mine, (grad_query * SCALE).astype(jnp.bfloat16), out_ref[0, rows, window]
-        )
+            grad_query = 0.0
+        if following:
+            block, found = (later_block, later)
 
     @pl.when(head == pl.num_programs(1) - 1)
     def write():
@@ -298,6 +332,98 @@
     return scale_rows * (
         scaled_grad - normed_unit * jnp.mean(scaled_grad * normed_unit, axis=-1, keepdims=True)
     )
+
+
+def norm_kernel(core_ref, own_ref, other_ref, gain_ref, out_ref):
+    def write(source):
+        rows = source[0].astype(jnp.float32)
+        scale = lax.rsqrt(jnp.mean(rows * rows, axis=-1, keepdims=True) + NORM_EPS)
+        out_ref[0] = (rows * scale * gain_ref[...]).astype(jnp.bfloat16)
+
+    @pl.when(pl.program_id(1) == 0)
+    def own():
+        write(own_ref)
+
+    @pl.when(pl.program_id(1) == 1)
+    def other():
+        write(other_ref)
+
+
+def norm_all(own, other, gain, core):
+    micro, rows, width = own.shape
+    cuts = 2
+    block = (1, rows // cuts, width)
+
+    def source(which):
+        return lambda m, s, i, core_ref: (m, jnp.where(s == which, i, (cuts - 1) * (1 - which)), 0)
+
+    def target(m, s, i, core_ref):
+        return (m, jnp.where(s == 0, core_ref[0], 1 - core_ref[0]) * cuts + i, 0)
+
+    return pl.pallas_call(
+        norm_kernel,
+        grid_spec=pltpu.PrefetchScalarGridSpec(
+            num_scalar_prefetch=1,
+            grid=(micro, 2, cuts),
+            in_specs=[
+                pl.BlockSpec(block, source(0)),
+                pl.BlockSpec(block, source(1)),
+                pl.BlockSpec((1, width), lambda m, s, i, core_ref: (0, 0)),
+            ],
+            out_specs=pl.BlockSpec(block, target),
+        ),
+        out_shape=jax.ShapeDtypeStruct((micro, 2 * rows, width), jnp.bfloat16),
+        compiler_params=pltpu.CompilerParams(vmem_limit_bytes=48 << 20),
+        cost_estimate=pl.CostEstimate(
+            flops=8 * micro * rows * width, bytes_accessed=8 * micro * rows * width, transcendentals=0
+        ),
+    )(core.reshape(1), own, other, gain[None])
+
+
+def token_grad_kernel(core_ref, part_ref, back_ref, token_ref, hidden_ref, gain_ref, out_ref, sum_ref):
+    rows = token_ref[0].astype(jnp.float32)
+    scale = lax.rsqrt(jnp.mean(rows * rows, axis=-1, keepdims=True) + NORM_EPS)
+    unit = rows * scale
+    grad = part_ref[0].astype(jnp.float32) + back_ref[0].astype(jnp.float32)
+    back = norm_back(grad, unit, scale, gain_ref[...])
+    out_ref[0] = (hidden_ref[0] + back).astype(jnp.bfloat16)
+
+    @pl.when((pl.program_id(0) == 0) & (pl.program_id(1) == 0))
+    def clear():
+        sum_ref[...] = jnp.zeros_like(sum_ref)
+
+    sum_ref[0:1] += jnp.sum(grad * unit, axis=0, keepdims=True)
+
+
+def token_grads(part, back, tokens, hidden, gain, core):
+    micro, rows, width = tokens.shape
+    cuts = 2
+    block = (1, rows // cuts, width)
+    here = pl.BlockSpec(block, lambda m, i, core_ref: (m, i, 0))
+    token_rows, sums = pl.pallas_call(
+        token_grad_kernel,
+        grid_spec=pltpu.PrefetchScalarGridSpec(
+            num_scalar_prefetch=1,
+            grid=(micro, cuts),
+            in_specs=[
+                pl.BlockSpec(block, lambda m, i, core_ref: (m, core_ref[0] * cuts + i, 0)),
+                here,
+                here,
+                here,
+                pl.BlockSpec((1, width), lambda m, i, core_ref: (0, 0)),
+            ],
+            out_specs=[here, pl.BlockSpec((8, width), lambda m, i, core_ref: (0, 0))],
+        ),
+        out_shape=[
+            jax.ShapeDtypeStruct(tokens.shape, jnp.bfloat16),
+            jax.ShapeDtypeStruct((8, width), jnp.float32),
+        ],
+        compiler_params=pltpu.CompilerParams(vmem_limit_bytes=48 << 20),
+        cost_estimate=pl.CostEstimate(
+            flops=20 * micro * rows * width, bytes_accessed=12 * micro * rows * width, transcendentals=0
+        ),
+    )(core.reshape(1), part, back, tokens, hidden, gain[None])
+    return (token_rows, sums[0])
 
 
 def adam_update(master, first, second, grad, rate, decay):
@@ -1159,7 +1285,6 @@
             jnp.concatenate([other, own], axis=axis),
         )
 
-    all_tokens = by_core(own_tokens, other_tokens, 1)
     gain_one = gain_low[0].astype(jnp.float32)
     gain_two = gain_low[1].astype(jnp.float32)
 
@@ -1167,8 +1292,7 @@
         scale = lax.rsqrt(jnp.mean(values * values, axis=-1, keepdims=True) + NORM_EPS)
         return (values * scale, scale)
 
-    normed_one = (unit(all_tokens.astype(jnp.float32))[0] * gain_one).astype(jnp.bfloat16)
-    normed_one = lax.optimization_barrier(normed_one)
+    normed_one = norm_all(own_tokens, other_tokens, gain_one, core)
     qkv = product(normed_one, qkv_weight, "mtd,de->mte").astype(jnp.bfloat16)
     attended_half, lse = attend(qkv, limit, branch)
     attended = by_core(
@@ -1210,14 +1334,10 @@
     early = grad_qkv.astype(jnp.bfloat16)
 
     grad_normed_part = product(grad_qkv_rows, qkv_weight, "mte,de->mtd").astype(jnp.bfloat16)
-    grad_normed_one = mine(grad_normed_part, 1, rows, core).astype(jnp.float32) + partner(
-        mine(grad_normed_part, 1, rows, 1 - core)
-    ).astype(jnp.float32)
-    unit_one, scale_one = unit(residual)
-    gain_one_grad = jnp.sum(grad_normed_one * unit_one, axis=(0, 1))
-    token_rows = (
-        grad_hidden_one + norm_back(grad_normed_one, unit_one, scale_one, gain_one)
-    ).astype(jnp.bfloat16)
+    grad_back = partner(mine(grad_normed_part, 1, rows, 1 - core))
+    token_rows, gain_one_grad = token_grads(
+        grad_normed_part, grad_back, own_tokens, grad_hidden_one, gain_one, core
+    )
     token_grad = transposed(token_rows)
     gain_grads = jnp.stack([gain_one_grad, gain_two_grad])
     late = (mine(late, 2, half, core).astype(jnp.float32) + late_back.astype(jnp.float32)).astype(

time: 848 us -> 825 us (0.973)
  other arithmetic: 75.7 us -> 45.5 us
    convert_element_type x2 -> x1, other arithmetic: 19.2 us -> 0.01 us  [step(): gain_one = gain_low[0].astype(jnp.float32)]
    pallas_call x0 -> x2, Pallas kernels: none -> 18.1 us  [the longest x1 9.37 us: norm_all(): pl.pallas_call(norm_kernel, grid_spec=pltpu.PrefetchScalarGridSpec(num_sc...]
    reduce_sum x3 -> x0, other arithmetic: 15.5 us -> none  [the longest x2 10.8 us: unit(): jnp.mean(values * values, axis=-1, keepdims=True) + NORM_EPS]
    pallas_call x1, Pallas kernels: 53.6 us -> 43.4 us  [attend(): pl.pallas_call(attend_kernel, grid=(micro, heads), in_specs=[column, colu...]
  transfers between devices with their start and end apart: 10 -> 10, of which waited for: 3 -> 3; matrix products, arithmetic and copies ran while one was open for 13% -> 11% of each run, Pallas kernels for 55% -> 58%
where the time goes in v2:
time: 825 us; the launch traced here: 818 us
  Pallas kernels  553 us (67%)
  matrix products  135 us (16%)
  other arithmetic  45.5 us (6%)
  local copies, waits for them, and re-layouts  42.4 us (5%)
  starting transfers between devices  17.9 us (2%)
  between operations  14.9 us (2%)
    pallas_call x2, Pallas kernels, gather_pieces(): pl.pallas_call(functools.partial(gather_kernel, split, base // 4 if split...  239 us
    pallas_call x1, Pallas kernels, reduce_slots(): pl.pallas_call(reduce_kernel, in_specs=[smem] * 2 + [vmem, hbm, hbm, vmem...  156 us
    dot_general x12, matrix products, product(): return jnp.einsum(spec, left, right, preferred_element_type=jnp.float32)  135 us
    pallas_call x1, Pallas kernels, attend_back(): pl.pallas_call(attend_back_kernel, grid=(micro, heads), in_specs=[row, ro...  80.8 us
    pallas_call x1, Pallas kernels, attend(): pl.pallas_call(attend_kernel, grid=(micro, heads), in_specs=[column, colu...  43.4 us
  transfers between devices with their start and end apart: 10, of which 3 were waited for; matrix products, arithmetic and copies ran while one was open for 11% of the time, Pallas kernels for 58%

profile of v2, /device:TPU:0, one launch (start us, length us, event | category | flops | bytes accessed | tf_op | source)
XLA Modules:
  0.0 818.2 jit_solution(11083562399105672873)
XLA Ops:
  9.4 785.3 %conditional.1 = (f32[16,64,1280]{2,1,0:T(8,128)}, f32[16,64,1280]{2,1,0:T(8,128)}, f32[16,64,1280]{2,1,0:T(8,128)}, bf16[2,1,704,1280]{3,2,0,1:T(8,128)(2,1)}, ...) conditional(s32[]{:T(128)} %bitcast.67, ...), branch_computations={%region_2.13_spmd, %region_13.30_spmd} | conditional | flops 164537630720 | bytes 1523107712 | solution.py:1241
  24.7 128.8 %branch_1_fun.8 = (bf16[1280,1920]{1,0:T(8,128)(2,1)}, bf16[1280,1280]{1,0:T(8,128)(2,1)S(1)}, bf16[1280,1280]{1,0:T(8,128)(2,1)}, bf16[1280,1280]{1,0:T(8,128)(2,1)}, f32[8,1280]{1,0:T(8,128)S(1)}) custom-call(s32[480]{0:T(512)S(1)} %reshape.567.block_ref, s32[480]{0:T(512)S(1)} %reshape.569.row_ref, s32[8]{0:T(128)S(1)} %get-tuple-element.295.spare_rank_ref, ...), custom_call_target="tpu_custom_call" | custom-call | bytes 157286400 | tf_op jit(solution)/shard_map/cond/branch_1_fun/pallas_call | solution.py:782
  165.8 9.4 %branch_1_fun.9 = bf16[2,1408,1280]{2,1,0:T(8,128)(2,1)} custom-call(s32[1]{0:T(128)} %bitcast.43.core_ref, bf16[2,704,1280]{2,1,0:T(8,128)(2,1)} %broadcast_select_fusion.1.own_ref.token_ref, bf16[2,704,1280]{2,1,0:T(8,128)(2,1)} %collective-permute-done.12.other_ref, f32[1,1280]{1,0:T(1,128)S(1)} %slice_convert_fusion.2.gain_ref), custom_call_target="tpu_custom_call" | custom-call | flops 14417920 | bytes 14417920 | tf_op jit(solution)/shard_map/cond/branch_1_fun/pallas_call | solution.py:363
  175.2 20.6 %convolution_convert_fusion.1.q_ref.k_ref.v_ref = bf16[2,1408,1920]{2,1,0:T(8,128)(2,1)} fusion(bf16[2,1408,1280]{2,1,0:T(8,128)(2,1)} %branch_1_fun.9, bf16[1280,1920]{1,0:T(8,128)(2,1)} %get-tuple-element.73), kind=kOutput, calls=%fused_computation.8 | convolution fusion | flops 13846609920 | bytes 22937600 | tf_op jit(solution)/shard_map/cond/branch_1_fun/mtd,de->mte/dot_general | solution.py:439
  195.8 43.4 %branch_1_fun.10 = (bf16[2,1408,640]{2,1,0:T(8,128)(2,1)S(1)}, f32[2,1408,128]{2,1,0:T(8,128)S(1)}) custom-call(s32[2,384,1]{2,1,0:T(8,128)S(1)} %reshape.649.limit_ref, s32[2,384,1]{2,1,0:T(8,128)S(1)} %reshape.650.branch_ref, bf16[2,1408,1920]{2,1,0:T(8,128)(2,1)} %convolution_convert_fusion.1.q_ref.k_ref.v_ref, ...), custom_call_target="tpu_custom_call" | custom-call | flops 24360517632 | bytes 14417920 | tf_op jit(solution)/shard_map/cond/branch_1_fun/pallas_call | solution.py:175
  249.1 8.8 %multiply_reduce_fusion.2 = (f32[2,704]{1,0:T(2,128)S(1)}, f32[2,704,1280]{2,1,0:T(8,128)S(1)}) fusion(bf16[1280,1280]{1,0:T(8,128)(2,1)S(1)} %copy-done.18, bf16[2,704,640]{2,1,0:T(8,128)(2,1)} %collective-permute-done.13, bf16[2,704,640]{2,1,0:T(8,128)(2,1)S(1)} %get-tuple-element.323, pred[]{:T(512)S(6)} %eq.148, ...), kind=kOutput, calls=%fused_computation.26 | convolution fusion | flops 4637161984 | bytes 17700352 | tf_op jit(solution)/shard_map/cond/branch_1_fun/mti,io->mto/dot_general | solution.py:439
  257.9 7.3 fusion.10
  265.3 9.6 %fusion.3 = bf16[1,1280,1280]{2,1,0:T(8,128)(2,1)} fusion(bf16[2,704,1280]{2,1,0:T(8,128)(2,1)S(1)} %broadcast_select_fusion, f32[2,704,1280]{2,1,0:T(8,128)} %fusion.10), kind=kOutput, calls=%fused_computation.28 | convolution fusion | flops 4624384000 | bytes 14090240 | tf_op jit(solution)/shard_map/cond/branch_1_fun/mti,mto->io/dot_general | solution.py:439
  274.8 8.1 multiply_convert_fusion
  284.8 7.6 fusion.4
  292.4 9.5 %multiply_reduce_fusion = (f32[1280]{0:T(1024)}, f32[2,704]{1,0:T(2,128)S(1)}, f32[2,704,1280]{2,1,0:T(8,128)S(1)}) fusion(f32[2,704,1280]{2,1,0:T(8,128)S(1)} %get-tuple-element.334, f32[2,704]{1,0:T(2,128)S(1)} %add_rsqrt_fusion, f32[1280]{0:T(1024)S(1)} %convert_reduce_fusion.1, bf16[2,704,1280]{2,1,0:T(8,128)(2,1)} %copy-done.84, ...), kind=kOutput, calls=%fused_computation.18 | convolution fusion | flops 4624545280 | bytes 21320704 | tf_op jit(solution)/shard_map/cond/branch_1_fun/mto,io->mti/dot_general | solution.py:439
  307.1 8.7 %fusion.5 = bf16[1,1280,1280]{2,1,0:T(8,128)(2,1)S(1)} fusion(bf16[2,704,1280]{2,1,0:T(8,128)(2,1)} %get-tuple-element.80, bf16[2,704,640]{2,1,0:T(8,128)(2,1)} %collective-permute-done.13, bf16[2,704,640]{2,1,0:T(8,128)(2,1)S(1)} %get-tuple-element.323, pred[]{:T(512)S(6)} %eq.148), kind=kOutput, calls=%fused_computation.30 | convolution fusion | flops 4631592960 | bytes 10485761 | tf_op jit(solution)/shard_map/cond/branch_1_fun/mti,mto->io/dot_general | solution.py:439
  320.7 5.2 convolution_convert_fusion.2
  335.9 80.8 %branch_1_fun.11 = bf16[2,1408,1920]{2,1,0:T(8,128)(2,1)} custom-call(s32[2,1,384]{2,1,0:T(1,128)} %reshape.647.limit_ref, s32[2,1,384]{2,1,0:T(1,128)} %reshape.648.branch_ref, f32[2,1408,128]{2,1,0:T(8,128)} %copy-done.19, bf16[2,1408,1920]{2,1,0:T(8,128)(2,1)} %convolution_convert_fusion.1.q_ref.k_ref.v_ref, ...), custom_call_target="tpu_custom_call" | custom-call | flops 56841207808 | bytes 25231360 | tf_op jit(solution)/shard_map/cond/branch_1_fun/pallas_call | solution.py:305
  416.7 17.5 %convolution_convert_fusion.part_ref = bf16[2,1408,1280]{2,1,0:T(8,128)(2,1)S(1)} fusion(bf16[2,1408,1920]{2,1,0:T(8,128)(2,1)} %branch_1_fun.11, bf16[1280,1920]{1,0:T(8,128)(2,1)S(1)} %bitcast.227), kind=kOutput, calls=%fused_computation.7 | convolution fusion | flops 13844807680 | bytes 22937600 | tf_op jit(solution)/shard_map/cond/branch_1_fun/mte,de->mtd/dot_general | solution.py:439
  440.0 5.4 constant_dynamic-slice_fusion
  446.2 10.8 %add_convert_fusion.1 = bf16[2,704,1280]{2,1,0:T(8,128)(2,1)} fusion(f32[2,704,1280]{2,1,0:T(8,128)S(1)} %bitcast.202, bf16[1280,1280]{1,0:T(8,128)(2,1)S(1)} %copy-done.82, f32[2,704,1280]{2,1,0:T(8,128)} %fusion.10), kind=kOutput, calls=%fused_computation.22 | convolution fusion | flops 4626350080 | bytes 21299200 | tf_op jit(solution)/shard_map/cond/branch_1_fun/mti,io->mto/dot_general | solution.py:439
  461.7 8.7 %branch_1_fun.12 = (bf16[2,704,1280]{2,1,0:T(8,128)(2,1)S(1)}, f32[8,1280]{1,0:T(8,128)S(1)}) custom-call(s32[1]{0:T(128)} %bitcast.43.core_ref, bf16[2,1408,1280]{2,1,0:T(8,128)(2,1)} %copy-done.22, bf16[2,704,1280]{2,1,0:T(8,128)(2,1)} %collective-permute-done.17.back_ref, bf16[2,704,1280]{2,1,0:T(8,128)(2,1)} %broadcast_select_fusion.1.own_ref.token_ref, ...), custom_call_target="tpu_custom_call" | custom-call | flops 36044800 | bytes 21626880 | tf_op jit(solution)/shard_map/cond/branch_1_fun/pallas_call | solution.py:403
  473.1 21.6 %bitcast_convert_fusion = bf16[1280,1920]{1,0:T(8,128)(2,1)} fusion(bf16[2,1408,1280]{2,1,0:T(8,128)(2,1)} %branch_1_fun.9, bf16[2,1408,1920]{2,1,0:T(8,128)(2,1)} %branch_1_fun.11), kind=kOutput, calls=%fused_computation.10 | convolution fusion | flops 13843660800 | bytes 22937600 | tf_op jit(solution)/shard_map/cond/branch_1_fun/mti,mto->io/dot_general | solution.py:439
  498.9 6.1 add_convert_fusion
  506.4 155.8 %branch_1_fun.13 = (bf16[16,4,16,1280]{3,2,1,0:T(8,128)(2,1)}, f32[8,1280]{1,0:T(8,128)}) custom-call(s32[544]{0:T(1024)} %reshape.557.source_ref, s32[8]{0:T(128)} %get-tuple-element.296.spare_ref, s32[8,1,640]{2,1,0:T(1,128)} %broadcast_in_dim.283.spare_mine_ref, bf16[80,16,1920]{2,1,0:T(8,128)(2,1)} %bitcast.205, bf16[3,80,16,640]{3,2,1,0:T(8,128)(2,1)} %bitcast.187, ...), custom_call_target="tpu_custom_call" | custom-call | bytes 78643200 | tf_op jit(solution)/shard_map/cond/branch_1_fun/pallas_call | solution.py:1135
  663.8 15.6 %branch_1_fun.14 = (f32[16,64,1280]{2,1,0:T(8,128)}, f32[16,64,1280]{2,1,0:T(8,128)}, f32[16,64,1280]{2,1,0:T(8,128)}, bf16[16,64,1280]{2,1,0:T(8,128)(2,1)}) custom-call(f32[16]{0:T(128)} %and_select_fusion.4.rate_ref, f32[16,64,1280]{2,1,0:T(8,128)} %get-tuple-element.66.master_ref, f32[16,64,1280]{2,1,0:T(8,128)} %get-tuple-element.82.first_ref, ...), custom_call_target="tpu_custom_call" | custom-call | flops 26214400 | bytes 36700160 | tf_op jit(solution)/shard_map/cond/branch_1_fun/pallas_call | solution.py:1220
  681.2 110.5 %branch_1_fun.15 = (bf16[6,1280,1280]{2,1,0:T(8,128)(2,1)}, f32[8,1280]{1,0:T(8,128)S(1)}) custom-call(s32[480]{0:T(512)S(1)} %copy-done.14, s32[480]{0:T(512)S(1)} %copy-done.12, s32[8]{0:T(128)S(1)} %copy-done.16, s32[8,1,1280]{2,1,0:T(1,128)S(1)} %copy-done.6, bf16[16,64,1280]{2,1,0:T(8,128)(2,1)S(1)} %copy-done.4, f32[8,1280]{1,0:T(8,128)S(1)} %concatenate.51.gain_ref), custom_call_target="tpu_custom_call" | custom-call | bytes 157286400 | tf_op jit(solution)/shard_map/cond/branch_1_fun/pallas_call | solution.py:782
  794.7 16.4 %copy.216 = bf16[6,1280,1280]{2,1,0:T(8,128)(2,1)} copy(bf16[6,1280,1280]{2,1,0:T(8,128)(2,1)} %get-tuple-element.392) | data formatting | bytes 39321600
  (219 shorter events, 81.5 us)
Async XLA Ops:
  14.0 139.6 %collective-permute-start.10 = (bf16[2,704,1280]{2,1,0:T(8,128)(2,1)}, bf16[2,704,1280]{2,1,0:T(8,128)(2,1)}, u32[]{:S(2)}, u32[]{:S(2)}) collective-permute-start(bf16[2,704,1280]{2,1,0:T(8,128)(2,1)} %bitcast.191), channel_id=1, source_target_pairs={{1,2},{2,1},{5,6},{6,5},{9,10},{10,9},{13,14},{14,13},{17,18},{18,... | collective-permute-start | bytes 10813448 | tf_op jit(solution)/shard_map/cond/branch_1_fun/ppermute | solution.py:40
  17.4 136.1 %copy-start.58 = (s32[120]{0:T(128)}, s32[120]{0:T(128)S(1)}, u32[]{:S(2)}) copy-start(s32[120]{0:T(128)S(1)} %convert_reduce_fusion) | copy-start | bytes 1444 | tf_op jit(solution)/shard_map/cond
  20.6 132.9 %copy-start.11 = (s32[480]{0:T(512)}, s32[480]{0:T(512)S(1)}, u32[]{:S(2)}) copy-start(s32[480]{0:T(512)S(1)} %reshape.569.row_ref) | copy-start | bytes 5764 | tf_op jit(solution)/shard_map/cond
  20.7 132.8 %copy-start.13 = (s32[480]{0:T(512)}, s32[480]{0:T(512)S(1)}, u32[]{:S(2)}) copy-start(s32[480]{0:T(512)S(1)} %reshape.567.block_ref) | copy-start | bytes 5764 | tf_op jit(solution)/shard_map/cond
  20.7 132.8 %copy-start.24 = (bf16[2,1,704,1280]{3,2,1,0:T(8,128)(2,1)S(1)}, bf16[2,1,704,1280]{3,2,1,0:T(8,128)(2,1)}, u32[]{:S(2)}) copy-start(bf16[2,1,704,1280]{3,2,1,0:T(8,128)(2,1)} %get-tuple-element.273) | copy-start | bytes 10813444 | tf_op jit(solution)/shard_map/cond
  24.6 131.6 %copy-start.15 = (s32[8]{0:T(128)}, s32[8]{0:T(128)S(1)}, u32[]{:S(2)}) copy-start(s32[8]{0:T(128)S(1)} %get-tuple-element.295.spare_rank_ref) | copy-start | bytes 100 | tf_op jit(solution)/shard_map/cond
  24.7 131.5 %copy-start.5 = (s32[8,1,1280]{2,1,0:T(1,128)}, s32[8,1,1280]{2,1,0:T(1,128)S(1)}, u32[]{:S(2)}) copy-start(s32[8,1,1280]{2,1,0:T(1,128)S(1)} %broadcast_in_dim.258.spare_mine_ref) | copy-start | bytes 122884 | tf_op jit(solution)/shard_map/cond
  156.4 9.4 %collective-permute-start.12 = (bf16[2,704,1280]{2,1,0:T(8,128)(2,1)}, bf16[2,704,1280]{2,1,0:T(8,128)(2,1)}, u32[]{:S(2)}, u32[]{:S(2)}) collective-permute-start(bf16[2,704,1280]{2,1,0:T(8,128)(2,1)} %broadcast_select_fusion.1.own_ref.token_ref), channel_id=1, source_target_pairs={{0,2},{2,0},{1,3},{3,1},{4,6},{6,4},{5,7},{7,5},{8,10},{10,8},{9,1... | collective-permute-start | bytes 10813448 | tf_op jit(solution)/shard_map/cond/branch_1_fun/ppermute | solution.py:52
  159.6 0.7 collective-permute-start.11
  162.1 83.4 %collective-permute-start.15 = (bf16[2,704,1280]{2,1,0:T(8,128)(2,1)}, bf16[2,704,1280]{2,1,0:T(8,128)(2,1)}, u32[]{:S(2)}, u32[]{:S(2)}) collective-permute-start(bf16[2,704,1280]{2,1,0:T(8,128)(2,1)} %bitcast.194), channel_id=1, source_target_pairs={{1,2},{2,1},{5,6},{6,5},{9,10},{10,9},{13,14},{14,13},{17,18},{18,... | collective-permute-start | bytes 10813448 | tf_op jit(solution)/shard_map/cond/branch_1_fun/ppermute | solution.py:40
  242.5 6.6 collective-permute-start.13
  257.9 44.1 %copy-start.27 = (f32[2,704,1280]{2,1,0:T(8,128)}, f32[2,704,1280]{2,1,0:T(8,128)S(1)}, u32[]{:S(2)}) copy-start(f32[2,704,1280]{2,1,0:T(8,128)S(1)} %get-tuple-element.334) | copy-start | bytes 21626884 | tf_op jit(solution)/shard_map/cond
  327.6 4.2 collective-permute-start.16
  331.8 84.9 %slice-start.7 = ((s8[4915200]{0:T(1024)(128)(4,1)}), s8[4194304]{0:T(1024)(128)(4,1)S(1)}, s32[]{:S(2)}) async-start(s8[4915200]{0:T(1024)(128)(4,1)} %bitcast.226), calls=%async_computation.12 | async-start | bytes 8388608 | tf_op jit(solution)/shard_map/cond
  335.9 80.8 %slice-start.8 = ((s8[4915200]{0:T(1024)(128)(4,1)}), s8[720896]{0:T(1024)(128)(4,1)S(1)}, s32[]{:S(2)}) async-start(s8[4915200]{0:T(1024)(128)(4,1)} %bitcast.226), calls=%async_computation.13 | async-start | bytes 1441792 | tf_op jit(solution)/shard_map/cond
  439.3 22.4 %collective-permute-start.17 = (bf16[2,704,1280]{2,1,0:T(8,128)(2,1)}, bf16[2,704,1280]{2,1,0:T(8,128)(2,1)}, u32[]{:S(2)}, u32[]{:S(2)}) collective-permute-start(bf16[2,704,1280]{2,1,0:T(8,128)(2,1)} %constant_dynamic-slice_fusion.1), channel_id=1, source_target_pairs={{0,2},{2,0},{1,3},{3,1},{4,6},{6,4},{5,7},{7,5},{8,10},{10,8},{9,1... | collective-permute-start | bytes 10813448 | tf_op jit(solution)/shard_map/cond/branch_1_fun/ppermute | solution.py:52
  445.4 53.5 %collective-permute-start.19 = (bf16[3,1280,640]{2,1,0:T(8,128)(2,1)}, bf16[3,1280,640]{2,1,0:T(8,128)(2,1)}, u32[]{:S(2)}, u32[]{:S(2)}) collective-permute-start(bf16[3,1280,640]{2,1,0:T(8,128)(2,1)} %constant_dynamic-slice_fusion), channel_id=1, source_target_pairs={{0,2},{2,0},{1,3},{3,1},{4,6},{6,4},{5,7},{7,5},{8,10},{10,8},{9,1... | collective-permute-start | bytes 14745608 | tf_op jit(solution)/shard_map/cond/branch_1_fun/ppermute | solution.py:52
  457.0 37.6 %collective-permute-start.14 = (bf16[2,704,1280]{2,1,0:T(8,128)(2,1)}, bf16[2,704,1280]{2,1,0:T(8,128)(2,1)}, u32[]{:S(2)}, u32[]{:S(2)}) collective-permute-start(bf16[2,704,1280]{2,1,0:T(8,128)(2,1)} %add_convert_fusion.1), channel_id=1, source_target_pairs={{1,2},{2,1},{5,6},{6,5},{9,10},{10,9},{13,14},{14,13},{17,18},{18,... | collective-permute-start | bytes 10813448 | tf_op jit(solution)/shard_map/cond/branch_1_fun/ppermute | solution.py:40
  461.7 37.2 %slice-start = ((s8[9830400]{0:T(1024)(128)(4,1)}), s8[1441792]{0:T(1024)(128)(4,1)S(1)}, s32[]{:S(2)}) async-start(s8[9830400]{0:T(1024)(128)(4,1)} %bitcast.182), calls=%async_computation.5 | async-start | bytes 2883584 | tf_op jit(solution)/shard_map/cond
  470.5 321.8 %collective-permute-start.18 = (bf16[2,704,1280]{2,1,0:T(8,128)(2,1)S(1)}, bf16[2,704,1280]{2,1,0:T(8,128)(2,1)}, u32[]{:S(2)}, u32[]{:S(2)}) collective-permute-start(bf16[2,704,1280]{2,1,0:T(8,128)(2,1)S(1)} %get-tuple-element.81), channel_id=1, source_target_pairs={{1,2},{2,1},{5,6},{6,5},{9,10},{10,9},{13,14},{14,13},{17,18},{18,... | collective-permute-start | bytes 10813448 | tf_op jit(solution)/shard_map/cond/branch_1_fun/ppermute | solution.py:40
  506.4 155.8 %copy-start.45 = (f32[2,1280]{1,0:T(2,128)S(1)}, f32[2,1280]{1,0:T(2,128)}, u32[]{:S(2)}) copy-start(f32[2,1280]{1,0:T(2,128)} %get-tuple-element.67) | copy-start | bytes 30724 | tf_op jit(solution)/shard_map/cond
  506.4 155.8 %copy-start.55 = (f32[2,1280]{1,0:T(2,128)S(1)}, f32[2,1280]{1,0:T(2,128)}, u32[]{:S(2)}) copy-start(f32[2,1280]{1,0:T(2,128)} %get-tuple-element.88) | copy-start | bytes 30724 | tf_op jit(solution)/shard_map/cond
  506.4 155.9 %copy-start.57 = (f32[2,1280]{1,0:T(2,128)S(1)}, f32[2,1280]{1,0:T(2,128)}, u32[]{:S(2)}) copy-start(f32[2,1280]{1,0:T(2,128)} %get-tuple-element.90) | copy-start | bytes 30724 | tf_op jit(solution)/shard_map/cond
  506.4 155.9 %copy-start.74 = (pred[2]{0:T(512)(128)(4,1)S(1)}, pred[2]{0:T(512)(128)(4,1)}, u32[]{:S(2)}) copy-start(pred[2]{0:T(512)(128)(4,1)} %copy-done.73) | copy-start | bytes 10 | tf_op jit(solution)/shard_map/cond
  (38 other events, 352.1 us)

commit v3 on v2

--- a/solution.py
+++ b/solution.py
@@ -137,15 +137,17 @@
             scores.append(raw)
         return scores
 
-    def weigh(scores, first, count, parts):
+    def weigh(scores):
+        top = functools.reduce(jnp.maximum, [jnp.max(s, axis=1, keepdims=True) for s in scores])
+        return (top, [jnp.exp2(raw - top).astype(jnp.bfloat16) for raw in scores])
+
+    def collect(weighed, first, count, parts):
+        top, weights = weighed
         rows = pl.ds(first, count)
-        top = functools.reduce(jnp.maximum, [jnp.max(s, axis=1, keepdims=True) for s in scores])
         gained = 0.0
-        for raw, (key_first, keys, kind) in zip(scores, parts):
+        for weight, (key_first, keys, kind) in zip(weights, parts):
             gained = gained + jnp.dot(
-                jnp.exp2(raw - top).astype(jnp.bfloat16),
-                values[key_first : key_first + keys],
-                preferred_element_type=jnp.float32,
+                weight, values[key_first : key_first + keys], preferred_element_type=jnp.float32
             )
         weight_sum = jnp.max(jnp.where(mine, 0.0, gained), axis=1, keepdims=True)
         gained = (gained * (1.0 / weight_sum)).astype(jnp.bfloat16)
@@ -156,10 +158,15 @@
 
     blocks = query_blocks(q_ref.shape[1])
     scores = score(*blocks[0])
-    for block, following in zip(blocks, blocks[1:] + [None]):
-        later = score(*following) if following else None
-        weigh(scores, *block)
+    weighed = None
+    for i in range(len(blocks)):
+        later = score(*blocks[i + 1]) if i + 1 < len(blocks) else None
+        before = weighed
+        weighed = weigh(scores)
+        if i:
+            collect(before, *blocks[i - 1])
         scores = later
+    collect(weighed, *blocks[-1])
 
 
 def attend(qkv, limit, branch):
@@ -240,8 +247,7 @@
             lax.dot_general(values_all[part], grad_less, NT, preferred_element_type=jnp.float32),
         )
 
-    def spread(found, part, kind, block):
-        query, grad, query_less, grad_less = block
+    def weigh(found, part, kind):
         raw, grad_prob = found
         prob = jnp.exp2(raw)
         if kind != "all":
@@ -254,10 +260,12 @@
                 branch_ref[0],
             )
             prob = jnp.where(ok, prob, 0.0)
-        grad_raw = (prob * grad_prob).astype(jnp.bfloat16)
-        dv_sum[part, window] += jnp.dot(
-            prob.astype(jnp.bfloat16), grad, preferred_element_type=jnp.float32
-        )
+        return (prob.astype(jnp.bfloat16), (prob * grad_prob).astype(jnp.bfloat16))
+
+    def collect(weighed, part, block):
+        prob, grad_raw = weighed
+        query, grad = block[:2]
+        dv_sum[part, window] += jnp.dot(prob, grad, preferred_element_type=jnp.float32)
         dk_sum[part, window] += jnp.dot(grad_raw, query, preferred_element_type=jnp.float32)
         return lax.dot_general(grad_raw, keys_all[part], TN, preferred_element_type=jnp.float32)
 
@@ -267,24 +275,34 @@
             for cut in range(key_first, key_first + keys, KEY_BLOCK):
                 part = slice(cut, min(cut + KEY_BLOCK, key_first + keys))
                 units.append((first, count, part, kind))
-    block = factors(*units[0][:2])
-    found = scores(units[0][2], block)
+    def finish(i, weighed, block, grad_query):
+        first, count, part, kind = units[i]
+        grad_query = grad_query + collect(weighed, part, block)
+        if i + 1 < len(units) and units[i + 1][0] == first:
+            return grad_query
+        rows = pl.ds(first, count)
+        out_ref[0, rows, window] = jnp.where(
+            mine, (grad_query * SCALE).astype(jnp.bfloat16), out_ref[0, rows, window]
+        )
+        return 0.0
+
+    held = {units[0][0]: factors(*units[0][:2])}
+    found = scores(units[0][2], held[units[0][0]])
+    weighed = None
     grad_query = 0.0
-    for unit, following in zip(units, units[1:] + [None]):
-        first, count, part, kind = unit
-        same = following and following[0] == first
-        if following:
-            later_block = block if same else factors(*following[:2])
-            later = scores(following[2], later_block)
-        grad_query = grad_query + spread(found, part, kind, block)
-        if not same:
-            rows = pl.ds(first, count)
-            out_ref[0, rows, window] = jnp.where(
-                mine, (grad_query * SCALE).astype(jnp.bfloat16), out_ref[0, rows, window]
-            )
-            grad_query = 0.0
-        if following:
-            block, found = (later_block, later)
+    for i, (first, count, part, kind) in enumerate(units):
+        later = None
+        if i + 1 < len(units):
+            following = units[i + 1]
+            if following[0] not in held:
+                held[following[0]] = factors(*following[:2])
+            later = scores(following[2], held[following[0]])
+        before = weighed
+        weighed = weigh(found, part, kind)
+        if i:
+            grad_query = finish(i - 1, before, held[units[i - 1][0]], grad_query)
+        found = later
+    finish(len(units) - 1, weighed, held[units[-1][0]], grad_query)
 
     @pl.when(head == pl.num_programs(1) - 1)
     def write():
@@ -656,7 +674,7 @@
     per_piece = piece // GROUP
     for i in range(base):
         source = pl.ds(i % per_piece * GROUP, GROUP)
-        whole[me, i] = low_ref[x * half + i // per_piece, source]
+        whole[me, i] = low_ref[x * half + i // per_piece, source].astype(jnp.bfloat16)
     greet()
 
     def window(first, count):
@@ -674,7 +692,7 @@
     gains.begin(gain_ref[...])
     count = SPARE // 2
     for i in range(count):
-        found = low_ref[spare_rank_ref[x * count + i]]
+        found = low_ref[spare_rank_ref[x * count + i]].astype(jnp.bfloat16)
         spare[pl.ds(i * piece, piece)] = jnp.where(spare_mine_ref[x * count + i] > 0, found, 0)
     rows = core_in.shape[0]
 
@@ -829,6 +847,7 @@
 
 def gather_slots(low, gains, owners, split):
     slots, piece, width = low.shape
+    low = low.astype(jnp.bfloat16)
     piece_owner, rank = owner_slots(owners, slots)
     rows = slots * piece
     half = -(-(rows // 2 + 1) // GROUP) * GROUP
@@ -932,8 +951,8 @@
     late_three,
     final,
     pair_in,
-    full,
-    full_in,
+    own_in,
+    other_in,
     spares,
     gain_sum,
     gain_in,
@@ -1035,18 +1054,13 @@
     ends = Flow()
     own_spare = spares.at[z, y, x, core]
     ends.push(final.at[pl.ds((1 - core) * owned, owned)], pair_in, sems[14:16], (0,), across("core"))
+    ends.push(final.at[pl.ds(core * owned, owned)], own_in, sems[14:16], (1,), across("x"))
     spares[z, y, x, core] = final[pl.ds(2 * owned, 2)]
     for d in range(1, depth):
         ends.push(own_spare, own_spare, sems[16:18], (d,), ahead(d))
     gain_out[...] = gains.result()
     ends.arrive(pair_in, sems[14:16], (0,))
-    for g in range(owned):
-        mine = final[core * owned + g]
-        theirs = pair_in[g]
-        first = core == 0
-        full[g, :, pl.ds(pl.multiple_of(core * narrow, LANES), narrow)] = mine
-        full[g, :, pl.ds(pl.multiple_of((1 - core) * narrow, LANES), narrow)] = theirs
-    ends.push(full, full_in, sems[14:16], (1,), across("x"))
+    ends.push(pair_in, other_in, sems[14:16], (5,), across("x"))
     for d in range(1, depth):
         from_z = spares.at[lax.rem(z - d + depth, depth), y, x, core]
         ends.arrive(from_z, sems[16:18], (d,))
@@ -1059,13 +1073,19 @@
     here = spares.at[:, :, :, core]
     ends.push(here, here, sems[14:16], (4,), across("core"))
     ends.arrive(spares.at[:, :, :, 1 - core], sems[14:16], (4,))
-    ends.arrive(full_in, sems[14:16], (1,))
+    ends.arrive(own_in, sems[14:16], (1,))
+    ends.arrive(other_in, sems[14:16], (5,))
     per_piece = slot_ref.shape[1]
     half = CAPACITY // 2
+    own_columns = pl.ds(pl.multiple_of(core * narrow, LANES), narrow)
+    other_columns = pl.ds(pl.multiple_of((1 - core) * narrow, LANES), narrow)
     for i in range(half):
         for g in range(per_piece):
-            slot_ref[x * half + i, g] = full[i * per_piece + g]
-            slot_ref[(1 - x) * half + i, g] = full_in[i * per_piece + g]
+            at = i * per_piece + g
+            slot_ref[x * half + i, g, :, own_columns] = final[core * owned + at]
+            slot_ref[x * half + i, g, :, other_columns] = pair_in[at]
+            slot_ref[(1 - x) * half + i, g, :, own_columns] = own_in[at]
+            slot_ref[(1 - x) * half + i, g, :, other_columns] = other_in[at]
 
     def pick(slot, carry):
         for g in range(per_piece):
@@ -1146,8 +1166,8 @@
         + [
             group_block(per_block),
             group_block(owned),
-            pltpu.VMEM((owned, GROUP, width), jnp.bfloat16),
-            pltpu.VMEM((owned, GROUP, width), jnp.bfloat16),
+            group_block(owned),
+            group_block(owned),
             group_block(depth, Y_CHIPS, 2, 2, subs),
         ]
         + total_scratch(3, depth, width)[:2]
@@ -1155,7 +1175,7 @@
         + total_scratch(3, depth, width)[2:]
         + flow_sems
         + flow_sems
-        + sem_pair(5)
+        + sem_pair(6)
         + sem_pair(depth),
         compiler_params=pltpu.CompilerParams(
             collective_id=2, has_side_effects=True, vmem_limit_bytes=56 << 20
@@ -1271,7 +1291,7 @@
     limit, branch = tail_limits(transposed(parents[:, 0]))
     arrived = moved(tokens[:, 0])
     qkv_weight, out_weight, up_weight, down_weight, gain_low = gather_store(
-        weight_store.astype(jnp.bfloat16), gain_store.astype(jnp.bfloat16), owners, True, few
+        weight_store, gain_store.astype(jnp.bfloat16), owners, True, few
     )
     gain_low, arrived, cot = lax.optimization_barrier((gain_low, arrived, cotangent[:, 0]))
     own_tokens = settled(tokens[:, 0], arrived)

time: 825 us -> 823 us (level)
  no operation moved by 1% of the time
where the time goes in v3:
time: 823 us; the launch traced here: 816 us
  Pallas kernels  552 us (67%)
  matrix products  135 us (16%)
  other arithmetic  44.3 us (5%)
  local copies, waits for them, and re-layouts  42.3 us (5%)
  starting transfers between devices  17.9 us (2%)
  between operations  14.9 us (2%)
    pallas_call x2, Pallas kernels, gather_pieces(): pl.pallas_call(functools.partial(gather_kernel, split, base // 4 if split...  244 us
    pallas_call x1, Pallas kernels, reduce_slots(): pl.pallas_call(reduce_kernel, in_specs=[smem] * 2 + [vmem, hbm, hbm, vmem...  152 us
    dot_general x12, matrix products, product(): return jnp.einsum(spec, left, right, preferred_element_type=jnp.float32)  135 us
    pallas_call x1, Pallas kernels, attend_back(): pl.pallas_call(attend_back_kernel, grid=(micro, heads), in_specs=[row, ro...  82 us
    pallas_call x1, Pallas kernels, attend(): pl.pallas_call(attend_kernel, grid=(micro, heads), in_specs=[column, colu...  40.7 us
  transfers between devices with their start and end apart: 10, of which 3 were waited for; matrix products, arithmetic and copies ran while one was open for 11% of the time, Pallas kernels for 58%

profile of v3, /device:TPU:0, one launch (start us, length us, event | category | flops | bytes accessed | tf_op | source)
XLA Modules:
  0.0 815.6 jit_solution(5166590390547209136)
XLA Ops:
  9.4 782.7 %conditional.1 = (f32[16,64,1280]{2,1,0:T(8,128)}, f32[16,64,1280]{2,1,0:T(8,128)}, f32[16,64,1280]{2,1,0:T(8,128)}, bf16[2,1,704,1280]{3,2,0,1:T(8,128)(2,1)}, ...) conditional(s32[]{:T(128)} %bitcast.67, ...), branch_computations={%region_2.13_spmd, %region_13.30_spmd} | conditional | flops 164537630720 | bytes 1523107712 | solution.py:1261
  23.3 130.7 %branch_1_fun.8 = (bf16[1280,1920]{1,0:T(8,128)(2,1)}, bf16[1280,1280]{1,0:T(8,128)(2,1)S(1)}, bf16[1280,1280]{1,0:T(8,128)(2,1)}, bf16[1280,1280]{1,0:T(8,128)(2,1)}, f32[8,1280]{1,0:T(8,128)S(1)}) custom-call(s32[480]{0:T(512)S(1)} %reshape.567.block_ref, s32[480]{0:T(512)S(1)} %reshape.569.row_ref, s32[8]{0:T(128)S(1)} %get-tuple-element.295.spare_rank_ref, ...), custom_call_target="tpu_custom_call" | custom-call | bytes 157286400 | tf_op jit(solution)/shard_map/cond/branch_1_fun/pallas_call | solution.py:800
  166.4 9.4 %branch_1_fun.9 = bf16[2,1408,1280]{2,1,0:T(8,128)(2,1)} custom-call(s32[1]{0:T(128)} %bitcast.43.core_ref, bf16[2,704,1280]{2,1,0:T(8,128)(2,1)} %broadcast_select_fusion.1.own_ref.token_ref, bf16[2,704,1280]{2,1,0:T(8,128)(2,1)} %collective-permute-done.12.other_ref, f32[1,1280]{1,0:T(1,128)S(1)} %slice_convert_fusion.2.gain_ref), custom_call_target="tpu_custom_call" | custom-call | flops 14417920 | bytes 14417920 | tf_op jit(solution)/shard_map/cond/branch_1_fun/pallas_call | solution.py:381
  175.7 20.6 %convolution_convert_fusion.1.q_ref.k_ref.v_ref = bf16[2,1408,1920]{2,1,0:T(8,128)(2,1)} fusion(bf16[2,1408,1280]{2,1,0:T(8,128)(2,1)} %branch_1_fun.9, bf16[1280,1920]{1,0:T(8,128)(2,1)} %get-tuple-element.73), kind=kOutput, calls=%fused_computation.8 | convolution fusion | flops 13846609920 | bytes 22937600 | tf_op jit(solution)/shard_map/cond/branch_1_fun/mtd,de->mte/dot_general | solution.py:457
  196.3 40.7 %branch_1_fun.10 = (bf16[2,1408,640]{2,1,0:T(8,128)(2,1)S(1)}, f32[2,1408,128]{2,1,0:T(8,128)S(1)}) custom-call(s32[2,384,1]{2,1,0:T(8,128)S(1)} %reshape.649.limit_ref, s32[2,384,1]{2,1,0:T(8,128)S(1)} %reshape.650.branch_ref, bf16[2,1408,1920]{2,1,0:T(8,128)(2,1)} %convolution_convert_fusion.1.q_ref.k_ref.v_ref, ...), custom_call_target="tpu_custom_call" | custom-call | flops 24360517632 | bytes 14417920 | tf_op jit(solution)/shard_map/cond/branch_1_fun/pallas_call | solution.py:182
  247.0 8.8 %multiply_reduce_fusion.2 = (f32[2,704]{1,0:T(2,128)S(1)}, f32[2,704,1280]{2,1,0:T(8,128)S(1)}) fusion(bf16[1280,1280]{1,0:T(8,128)(2,1)S(1)} %copy-done.18, bf16[2,704,640]{2,1,0:T(8,128)(2,1)} %collective-permute-done.13, bf16[2,704,640]{2,1,0:T(8,128)(2,1)S(1)} %get-tuple-element.323, pred[]{:T(512)S(6)} %eq.148, ...), kind=kOutput, calls=%fused_computation.26 | convolution fusion | flops 4637161984 | bytes 17700352 | tf_op jit(solution)/shard_map/cond/branch_1_fun/mti,io->mto/dot_general | solution.py:457
  255.8 7.3 fusion.10
  263.1 9.6 %fusion.3 = bf16[1,1280,1280]{2,1,0:T(8,128)(2,1)} fusion(bf16[2,704,1280]{2,1,0:T(8,128)(2,1)S(1)} %broadcast_select_fusion, f32[2,704,1280]{2,1,0:T(8,128)} %fusion.10), kind=kOutput, calls=%fused_computation.28 | convolution fusion | flops 4624384000 | bytes 14090240 | tf_op jit(solution)/shard_map/cond/branch_1_fun/mti,mto->io/dot_general | solution.py:457
  272.7 8.1 multiply_convert_fusion
  282.7 7.6 fusion.4
  290.3 9.5 %multiply_reduce_fusion = (f32[1280]{0:T(1024)}, f32[2,704]{1,0:T(2,128)S(1)}, f32[2,704,1280]{2,1,0:T(8,128)S(1)}) fusion(f32[2,704,1280]{2,1,0:T(8,128)S(1)} %get-tuple-element.334, f32[2,704]{1,0:T(2,128)S(1)} %add_rsqrt_fusion, f32[1280]{0:T(1024)S(1)} %convert_reduce_fusion.1, bf16[2,704,1280]{2,1,0:T(8,128)(2,1)} %copy-done.82, ...), kind=kOutput, calls=%fused_computation.18 | convolution fusion | flops 4624545280 | bytes 21320704 | tf_op jit(solution)/shard_map/cond/branch_1_fun/mto,io->mti/dot_general | solution.py:457
  305.0 8.7 %fusion.5 = bf16[1,1280,1280]{2,1,0:T(8,128)(2,1)S(1)} fusion(bf16[2,704,1280]{2,1,0:T(8,128)(2,1)} %get-tuple-element.80, bf16[2,704,640]{2,1,0:T(8,128)(2,1)} %collective-permute-done.13, bf16[2,704,640]{2,1,0:T(8,128)(2,1)S(1)} %get-tuple-element.323, pred[]{:T(512)S(6)} %eq.148), kind=kOutput, calls=%fused_computation.30 | convolution fusion | flops 4631592960 | bytes 10485761 | tf_op jit(solution)/shard_map/cond/branch_1_fun/mti,mto->io/dot_general | solution.py:457
  318.6 5.2 convolution_convert_fusion.2
  333.7 82.0 %branch_1_fun.11 = bf16[2,1408,1920]{2,1,0:T(8,128)(2,1)} custom-call(s32[2,1,384]{2,1,0:T(1,128)} %reshape.647.limit_ref, s32[2,1,384]{2,1,0:T(1,128)} %reshape.648.branch_ref, f32[2,1408,128]{2,1,0:T(8,128)} %copy-done.19, bf16[2,1408,1920]{2,1,0:T(8,128)(2,1)} %convolution_convert_fusion.1.q_ref.k_ref.v_ref, ...), custom_call_target="tpu_custom_call" | custom-call | flops 56841207808 | bytes 25231360 | tf_op jit(solution)/shard_map/cond/branch_1_fun/pallas_call | solution.py:323
  415.7 17.5 %convolution_convert_fusion.part_ref = bf16[2,1408,1280]{2,1,0:T(8,128)(2,1)S(1)} fusion(bf16[2,1408,1920]{2,1,0:T(8,128)(2,1)} %branch_1_fun.11, bf16[1280,1920]{1,0:T(8,128)(2,1)S(1)} %bitcast.227), kind=kOutput, calls=%fused_computation.7 | convolution fusion | flops 13844807680 | bytes 22937600 | tf_op jit(solution)/shard_map/cond/branch_1_fun/mte,de->mtd/dot_general | solution.py:457
  439.0 5.4 constant_dynamic-slice_fusion
  445.2 10.8 %add_convert_fusion.1 = bf16[2,704,1280]{2,1,0:T(8,128)(2,1)} fusion(f32[2,704,1280]{2,1,0:T(8,128)S(1)} %bitcast.202, bf16[1280,1280]{1,0:T(8,128)(2,1)S(1)} %copy-done.80, f32[2,704,1280]{2,1,0:T(8,128)} %fusion.10), kind=kOutput, calls=%fused_computation.22 | convolution fusion | flops 4626350080 | bytes 21299200 | tf_op jit(solution)/shard_map/cond/branch_1_fun/mti,io->mto/dot_general | solution.py:457
  460.7 8.7 %branch_1_fun.12 = (bf16[2,704,1280]{2,1,0:T(8,128)(2,1)S(1)}, f32[8,1280]{1,0:T(8,128)S(1)}) custom-call(s32[1]{0:T(128)} %bitcast.43.core_ref, bf16[2,1408,1280]{2,1,0:T(8,128)(2,1)} %copy-done.22, bf16[2,704,1280]{2,1,0:T(8,128)(2,1)} %collective-permute-done.17.back_ref, bf16[2,704,1280]{2,1,0:T(8,128)(2,1)} %broadcast_select_fusion.1.own_ref.token_ref, ...), custom_call_target="tpu_custom_call" | custom-call | flops 36044800 | bytes 21626880 | tf_op jit(solution)/shard_map/cond/branch_1_fun/pallas_call | solution.py:421
  472.0 21.6 %bitcast_convert_fusion = bf16[1280,1920]{1,0:T(8,128)(2,1)} fusion(bf16[2,1408,1280]{2,1,0:T(8,128)(2,1)} %branch_1_fun.9, bf16[2,1408,1920]{2,1,0:T(8,128)(2,1)} %branch_1_fun.11), kind=kOutput, calls=%fused_computation.10 | convolution fusion | flops 13843660800 | bytes 22937600 | tf_op jit(solution)/shard_map/cond/branch_1_fun/mti,mto->io/dot_general | solution.py:457
  497.9 6.1 add_convert_fusion
  505.4 152.0 %branch_1_fun.13 = (bf16[16,4,16,1280]{3,2,1,0:T(8,128)(2,1)}, f32[8,1280]{1,0:T(8,128)}) custom-call(s32[544]{0:T(1024)} %reshape.557.source_ref, s32[8]{0:T(128)} %get-tuple-element.296.spare_ref, s32[8,1,640]{2,1,0:T(1,128)} %broadcast_in_dim.283.spare_mine_ref, bf16[80,16,1920]{2,1,0:T(8,128)(2,1)} %bitcast.205, bf16[3,80,16,640]{3,2,1,0:T(8,128)(2,1)} %bitcast.187, ...), custom_call_target="tpu_custom_call" | custom-call | bytes 78643200 | tf_op jit(solution)/shard_map/cond/branch_1_fun/pallas_call | solution.py:1155
  658.9 15.6 %branch_1_fun.14 = (f32[16,64,1280]{2,1,0:T(8,128)}, f32[16,64,1280]{2,1,0:T(8,128)}, f32[16,64,1280]{2,1,0:T(8,128)}, bf16[16,64,1280]{2,1,0:T(8,128)(2,1)}) custom-call(f32[16]{0:T(128)} %and_select_fusion.4.rate_ref, f32[16,64,1280]{2,1,0:T(8,128)} %get-tuple-element.66.low_ref.master_ref, f32[16,64,1280]{2,1,0:T(8,128)} %get-tuple-element.82.first_ref, ...), custom_call_target="tpu_custom_call" | custom-call | flops 26214400 | bytes 36700160 | tf_op jit(solution)/shard_map/cond/branch_1_fun/pallas_call | solution.py:1240
  676.3 112.8 %branch_1_fun.15 = (bf16[6,1280,1280]{2,1,0:T(8,128)(2,1)}, f32[8,1280]{1,0:T(8,128)S(1)}) custom-call(s32[480]{0:T(512)S(1)} %copy-done.14, s32[480]{0:T(512)S(1)} %copy-done.12, s32[8]{0:T(128)S(1)} %copy-done.16, s32[8,1,1280]{2,1,0:T(1,128)S(1)} %copy-done.6, bf16[16,64,1280]{2,1,0:T(8,128)(2,1)S(1)} %copy-done.4, f32[8,1280]{1,0:T(8,128)S(1)} %concatenate.51.gain_ref), custom_call_target="tpu_custom_call" | custom-call | bytes 157286400 | tf_op jit(solution)/shard_map/cond/branch_1_fun/pallas_call | solution.py:800
  792.1 16.4 %copy.216 = bf16[6,1280,1280]{2,1,0:T(8,128)(2,1)} copy(bf16[6,1280,1280]{2,1,0:T(8,128)(2,1)} %get-tuple-element.392) | data formatting | bytes 39321600
  (214 shorter events, 80.2 us)
Async XLA Ops:
  13.8 140.2 %collective-permute-start.10 = (bf16[2,704,1280]{2,1,0:T(8,128)(2,1)}, bf16[2,704,1280]{2,1,0:T(8,128)(2,1)}, u32[]{:S(2)}, u32[]{:S(2)}) collective-permute-start(bf16[2,704,1280]{2,1,0:T(8,128)(2,1)} %bitcast.191), channel_id=1, source_target_pairs={{1,2},{2,1},{5,6},{6,5},{9,10},{10,9},{13,14},{14,13},{17,18},{18,... | collective-permute-start | bytes 10813448 | tf_op jit(solution)/shard_map/cond/branch_1_fun/ppermute | solution.py:40
  17.2 139.6 %copy-start.57 = (s32[120]{0:T(128)}, s32[120]{0:T(128)S(1)}, u32[]{:S(2)}) copy-start(s32[120]{0:T(128)S(1)} %convert_reduce_fusion) | copy-start | bytes 1444 | tf_op jit(solution)/shard_map/cond
  20.4 136.3 %copy-start.11 = (s32[480]{0:T(512)}, s32[480]{0:T(512)S(1)}, u32[]{:S(2)}) copy-start(s32[480]{0:T(512)S(1)} %reshape.569.row_ref) | copy-start | bytes 5764 | tf_op jit(solution)/shard_map/cond
  20.5 136.2 %copy-start.13 = (s32[480]{0:T(512)}, s32[480]{0:T(512)S(1)}, u32[]{:S(2)}) copy-start(s32[480]{0:T(512)S(1)} %reshape.567.block_ref) | copy-start | bytes 5764 | tf_op jit(solution)/shard_map/cond
  20.6 133.5 %copy-start.24 = (bf16[2,1,704,1280]{3,2,1,0:T(8,128)(2,1)S(1)}, bf16[2,1,704,1280]{3,2,1,0:T(8,128)(2,1)}, u32[]{:S(2)}) copy-start(bf16[2,1,704,1280]{3,2,1,0:T(8,128)(2,1)} %get-tuple-element.273) | copy-start | bytes 10813444 | tf_op jit(solution)/shard_map/cond
  23.2 133.6 %copy-start.15 = (s32[8]{0:T(128)}, s32[8]{0:T(128)S(1)}, u32[]{:S(2)}) copy-start(s32[8]{0:T(128)S(1)} %get-tuple-element.295.spare_rank_ref) | copy-start | bytes 100 | tf_op jit(solution)/shard_map/cond
  23.3 133.5 %copy-start.5 = (s32[8,1,1280]{2,1,0:T(1,128)}, s32[8,1,1280]{2,1,0:T(1,128)S(1)}, u32[]{:S(2)}) copy-start(s32[8,1,1280]{2,1,0:T(1,128)S(1)} %broadcast_in_dim.258.spare_mine_ref) | copy-start | bytes 122884 | tf_op jit(solution)/shard_map/cond
  156.9 9.4 %collective-permute-start.12 = (bf16[2,704,1280]{2,1,0:T(8,128)(2,1)}, bf16[2,704,1280]{2,1,0:T(8,128)(2,1)}, u32[]{:S(2)}, u32[]{:S(2)}) collective-permute-start(bf16[2,704,1280]{2,1,0:T(8,128)(2,1)} %broadcast_select_fusion.1.own_ref.token_ref), channel_id=1, source_target_pairs={{0,2},{2,0},{1,3},{3,1},{4,6},{6,4},{5,7},{7,5},{8,10},{10,8},{9,1... | collective-permute-start | bytes 10813448 | tf_op jit(solution)/shard_map/cond/branch_1_fun/ppermute | solution.py:52
  160.2 0.7 collective-permute-start.11
  162.7 80.7 %collective-permute-start.15 = (bf16[2,704,1280]{2,1,0:T(8,128)(2,1)}, bf16[2,704,1280]{2,1,0:T(8,128)(2,1)}, u32[]{:S(2)}, u32[]{:S(2)}) collective-permute-start(bf16[2,704,1280]{2,1,0:T(8,128)(2,1)} %bitcast.194), channel_id=1, source_target_pairs={{1,2},{2,1},{5,6},{6,5},{9,10},{10,9},{13,14},{14,13},{17,18},{18,... | collective-permute-start | bytes 10813448 | tf_op jit(solution)/shard_map/cond/branch_1_fun/ppermute | solution.py:40
  240.4 6.7 collective-permute-start.13
  255.8 44.1 %copy-start.27 = (f32[2,704,1280]{2,1,0:T(8,128)}, f32[2,704,1280]{2,1,0:T(8,128)S(1)}, u32[]{:S(2)}) copy-start(f32[2,704,1280]{2,1,0:T(8,128)S(1)} %get-tuple-element.334) | copy-start | bytes 21626884 | tf_op jit(solution)/shard_map/cond
  325.4 4.2 collective-permute-start.16
  329.6 86.0 %slice-start.7 = ((s8[4915200]{0:T(1024)(128)(4,1)}), s8[4194304]{0:T(1024)(128)(4,1)S(1)}, s32[]{:S(2)}) async-start(s8[4915200]{0:T(1024)(128)(4,1)} %bitcast.226), calls=%async_computation.12 | async-start | bytes 8388608 | tf_op jit(solution)/shard_map/cond
  333.7 82.0 %slice-start.8 = ((s8[4915200]{0:T(1024)(128)(4,1)}), s8[720896]{0:T(1024)(128)(4,1)S(1)}, s32[]{:S(2)}) async-start(s8[4915200]{0:T(1024)(128)(4,1)} %bitcast.226), calls=%async_computation.13 | async-start | bytes 1441792 | tf_op jit(solution)/shard_map/cond
  438.3 22.4 %collective-permute-start.17 = (bf16[2,704,1280]{2,1,0:T(8,128)(2,1)}, bf16[2,704,1280]{2,1,0:T(8,128)(2,1)}, u32[]{:S(2)}, u32[]{:S(2)}) collective-permute-start(bf16[2,704,1280]{2,1,0:T(8,128)(2,1)} %constant_dynamic-slice_fusion.1), channel_id=1, source_target_pairs={{0,2},{2,0},{1,3},{3,1},{4,6},{6,4},{5,7},{7,5},{8,10},{10,8},{9,1... | collective-permute-start | bytes 10813448 | tf_op jit(solution)/shard_map/cond/branch_1_fun/ppermute | solution.py:52
  444.4 53.5 %collective-permute-start.19 = (bf16[3,1280,640]{2,1,0:T(8,128)(2,1)}, bf16[3,1280,640]{2,1,0:T(8,128)(2,1)}, u32[]{:S(2)}, u32[]{:S(2)}) collective-permute-start(bf16[3,1280,640]{2,1,0:T(8,128)(2,1)} %constant_dynamic-slice_fusion), channel_id=1, source_target_pairs={{0,2},{2,0},{1,3},{3,1},{4,6},{6,4},{5,7},{7,5},{8,10},{10,8},{9,1... | collective-permute-start | bytes 14745608 | tf_op jit(solution)/shard_map/cond/branch_1_fun/ppermute | solution.py:52
  456.0 37.7 %collective-permute-start.14 = (bf16[2,704,1280]{2,1,0:T(8,128)(2,1)}, bf16[2,704,1280]{2,1,0:T(8,128)(2,1)}, u32[]{:S(2)}, u32[]{:S(2)}) collective-permute-start(bf16[2,704,1280]{2,1,0:T(8,128)(2,1)} %add_convert_fusion.1), channel_id=1, source_target_pairs={{1,2},{2,1},{5,6},{6,5},{9,10},{10,9},{13,14},{14,13},{17,18},{18,... | collective-permute-start | bytes 10813448 | tf_op jit(solution)/shard_map/cond/branch_1_fun/ppermute | solution.py:40
  460.7 37.2 %slice-start = ((s8[9830400]{0:T(1024)(128)(4,1)}), s8[1441792]{0:T(1024)(128)(4,1)S(1)}, s32[]{:S(2)}) async-start(s8[9830400]{0:T(1024)(128)(4,1)} %bitcast.182), calls=%async_computation.5 | async-start | bytes 2883584 | tf_op jit(solution)/shard_map/cond
  469.4 320.3 %collective-permute-start.18 = (bf16[2,704,1280]{2,1,0:T(8,128)(2,1)S(1)}, bf16[2,704,1280]{2,1,0:T(8,128)(2,1)}, u32[]{:S(2)}, u32[]{:S(2)}) collective-permute-start(bf16[2,704,1280]{2,1,0:T(8,128)(2,1)S(1)} %get-tuple-element.81), channel_id=1, source_target_pairs={{1,2},{2,1},{5,6},{6,5},{9,10},{10,9},{13,14},{14,13},{17,18},{18,... | collective-permute-start | bytes 10813448 | tf_op jit(solution)/shard_map/cond/branch_1_fun/ppermute | solution.py:40
  505.4 152.0 %copy-start.44 = (f32[2,1280]{1,0:T(2,128)S(1)}, f32[2,1280]{1,0:T(2,128)}, u32[]{:S(2)}) copy-start(f32[2,1280]{1,0:T(2,128)} %get-tuple-element.67) | copy-start | bytes 30724 | tf_op jit(solution)/shard_map/cond
  505.4 152.0 %copy-start.54 = (f32[2,1280]{1,0:T(2,128)S(1)}, f32[2,1280]{1,0:T(2,128)}, u32[]{:S(2)}) copy-start(f32[2,1280]{1,0:T(2,128)} %get-tuple-element.88) | copy-start | bytes 30724 | tf_op jit(solution)/shard_map/cond
  505.4 152.0 %copy-start.56 = (f32[2,1280]{1,0:T(2,128)S(1)}, f32[2,1280]{1,0:T(2,128)}, u32[]{:S(2)}) copy-start(f32[2,1280]{1,0:T(2,128)} %get-tuple-element.90) | copy-start | bytes 30724 | tf_op jit(solution)/shard_map/cond
  505.4 152.0 %copy-start.72 = (pred[2]{0:T(512)(128)(4,1)S(1)}, pred[2]{0:T(512)(128)(4,1)}, u32[]{:S(2)}) copy-start(pred[2]{0:T(512)(128)(4,1)} %copy-done.71) | copy-start | bytes 10 | tf_op jit(solution)/shard_map/cond
  (36 other events, 333.4 us)
